TPU v7x, 32 devices: a whole 2x2x4 slice. The times are simulated.
32 devices in a mesh: dp: 4 (over y, x), expert: 8 (over z, core).
Axes of the slice: x: 2, y: 2, z: 4, core: 2. Of those that a mesh axis runs over, the one named last changes fastest.
Arguments:
- tokens: bfloat16 [256, 2048], P('dp'), may hold values from -6 to 6
- d_mixed: bfloat16 [256, 2048], P('dp'), may hold values from -6 to 6
- route_ids: int32 [256, 6], replicated, may hold values from 0 to 15, all different within a row; in each aligned block of 64 rows (0 to 63, 64 to 127, ...) at most 64 rows name the same one
- route_weight: float32 [256, 6], replicated, may hold values from 0.05 to 1
- gate_weight: bfloat16 [32, 704, 2048], P(('expert', 'dp')), may hold values from -0.125 to 0.125
- up_weight: bfloat16 [32, 704, 2048], P(('expert', 'dp')), may hold values from -0.125 to 0.125
- down_weight: bfloat16 [32, 704, 2048], P(('expert', 'dp')), may hold values from -0.15625 to 0.15625
Outputs:
- mixed: bfloat16 [256, 2048], P('dp')
- d_route: float32 [256, 6], P('dp')
- d_tokens: bfloat16 [256, 2048], P('dp')
- grad_gate: bfloat16 [32, 704, 2048], P(('expert', 'dp'))
- grad_up: bfloat16 [32, 704, 2048], P(('expert', 'dp'))
- grad_down: bfloat16 [32, 704, 2048], P(('expert', 'dp'))
Inputs may be any that keep to these rules, and one draw needn't show every extreme that they name: `route_ids`: each row names 6 different experts. In each aligned block of 64 rows (the tokens of one index of dp) no expert is named by more than 64 rows, and in every draw some expert is named by exactly 64 rows of some block.
All inputs are finite; a program needn't handle non-finite values.
Results may differ from a plain program's by a relative error of at most 0.0064.
Values may be sent and summed in bfloat16 or wider, within the bound.
A program may use at most 64 MiB of HBM per device.

v0:
```python
import jax
import jax.numpy as jnp
from jax import lax
from jax.sharding import PartitionSpec as P

EXP_DEV = 2


def slot_table(block_ids, expert_count):
    flat_ids = block_ids.reshape(-1)
    one_hot = (flat_ids[:, None] == jnp.arange(expert_count, dtype=jnp.int32)[None, :]).astype(
        jnp.int32
    )
    earlier = jnp.cumsum(one_hot, axis=0) - one_hot
    return jnp.sum(earlier * one_hot, axis=1)


def selection(block_ids, block_weight, first_expert, expert_span, capacity, expert_count):
    flat_ids = block_ids.reshape(-1)
    slot_numbers = slot_table(block_ids, expert_count)
    offset_ids = flat_ids - first_expert
    inside_mask = (offset_ids >= 0) & (offset_ids < expert_span)
    target_row = jnp.where(inside_mask, offset_ids * capacity + slot_numbers, -1)
    matches = (
        target_row[None, :] == jnp.arange(expert_span * capacity, dtype=jnp.int32)[:, None]
    ).astype(jnp.float32)
    matches = matches.reshape(expert_span * capacity, block_ids.shape[0], block_ids.shape[1])
    chosen = jnp.sum(matches, axis=2)
    weighted = jnp.sum(matches * block_weight[None, :, :], axis=2)
    return (matches, chosen, weighted)


def contract_first(left, right):
    return lax.dot_general(
        left, right, (((0,), (0,)), ((), ())), preferred_element_type=jnp.float32
    )


def contract_last(left, right):
    return lax.dot_general(
        left, right, (((1,), (1,)), ((), ())), preferred_element_type=jnp.float32
    )


def body(tokens, d_mixed, route_ids, route_weight, gate_weight, up_weight, down_weight):
    dp_count = lax.axis_size("dp")
    dp_index = lax.axis_index("dp")
    column_index = lax.axis_index("expert")
    expert_count = EXP_DEV * lax.axis_size("expert")
    pieces = dp_count // EXP_DEV
    token_count = tokens.shape[0]
    model_width = tokens.shape[1]
    choice_count = route_ids.shape[1]
    capacity = min(token_count, max(8, 5 * token_count * choice_count // expert_count))
    which_local = dp_index // pieces
    first_expert = column_index * EXP_DEV
    id_blocks = route_ids.reshape(dp_count, token_count, choice_count)
    weight_blocks = route_weight.reshape(dp_count, token_count, choice_count)
    own_ids = lax.dynamic_index_in_dim(id_blocks, dp_index, 0, keepdims=False)
    own_weight = lax.dynamic_index_in_dim(weight_blocks, dp_index, 0, keepdims=False)
    matches, chosen, weighted = selection(
        own_ids, own_weight, first_expert, EXP_DEV, capacity, expert_count
    )
    row_total = dp_count * capacity
    all_in, all_grad = (
        lax.all_gather(tokens, "dp", axis=0, tiled=True),
        lax.all_gather(d_mixed, "dp", axis=0, tiled=True),
    )

    def pick_rows(block_ids, block_weight):
        unused, picked, picked_weight = selection(
            block_ids, block_weight, first_expert + which_local, 1, capacity, expert_count
        )
        return (picked, jnp.sum(picked_weight, axis=1))

    chosen_all, scale_all = jax.vmap(pick_rows)(id_blocks, weight_blocks)
    chosen_all = chosen_all.astype(jnp.bfloat16)
    in_blocks = all_in.reshape(dp_count, token_count, model_width)
    grad_blocks = all_grad.reshape(dp_count, token_count, model_width)
    routed_in = jnp.einsum(
        "sct,std->scd", chosen_all, in_blocks, preferred_element_type=jnp.float32
    )
    routed_in = routed_in.astype(jnp.bfloat16).reshape(row_total, model_width)
    routed_grad = scale_all[:, :, None] * jnp.einsum(
        "sct,std->scd", chosen_all, grad_blocks, preferred_element_type=jnp.float32
    )
    routed_grad = routed_grad.astype(jnp.bfloat16).reshape(row_total, model_width)
    gate_piece = gate_weight[0]
    up_piece = up_weight[0]
    down_piece = down_weight[0]
    gate_value = contract_last(routed_in, gate_piece)
    up_value = contract_last(routed_in, up_piece)
    sigmoid_gate = jax.nn.sigmoid(gate_value)
    activated = gate_value * sigmoid_gate
    hidden = (activated * up_value).astype(jnp.bfloat16)
    part_out = jnp.dot(hidden, down_piece, preferred_element_type=jnp.float32).astype(jnp.bfloat16)
    returned = lax.all_to_all(
        part_out.reshape(dp_count, capacity, model_width),
        "dp",
        split_axis=0,
        concat_axis=0,
        tiled=True,
    )
    expert_out = jnp.sum(
        returned.reshape(EXP_DEV, pieces, capacity, model_width).astype(jnp.float32), axis=1
    )
    expert_out = expert_out.reshape(EXP_DEV * capacity, model_width)
    mixed_part = jnp.dot(weighted.T, expert_out, precision=lax.Precision.HIGHEST)
    paired = jnp.dot(expert_out, d_mixed.astype(jnp.float32).T, precision=lax.Precision.HIGHEST)
    route_part = jnp.sum(matches * paired[:, :, None], axis=0)
    mixed_sum, route_sum = lax.psum((mixed_part, route_part), "expert")
    d_hidden = contract_last(routed_grad, down_piece)
    grad_down = contract_first(hidden, routed_grad).astype(jnp.bfloat16)
    d_gate_pre = (
        d_hidden * up_value * sigmoid_gate * (1.0 + gate_value * (1.0 - sigmoid_gate))
    ).astype(jnp.bfloat16)
    d_up_pre = (d_hidden * activated).astype(jnp.bfloat16)
    grad_gate = contract_first(d_gate_pre, routed_in).astype(jnp.bfloat16)
    grad_up = contract_first(d_up_pre, routed_in).astype(jnp.bfloat16)
    part_in = (
        jnp.dot(d_gate_pre, gate_piece, preferred_element_type=jnp.float32)
        + jnp.dot(d_up_pre, up_piece, preferred_element_type=jnp.float32)
    ).astype(jnp.bfloat16)
    returned_in = lax.all_to_all(
        part_in.reshape(dp_count, capacity, model_width),
        "dp",
        split_axis=0,
        concat_axis=0,
        tiled=True,
    )
    expert_in = jnp.sum(
        returned_in.reshape(EXP_DEV, pieces, capacity, model_width).astype(jnp.float32), axis=1
    )
    expert_in = expert_in.reshape(EXP_DEV * capacity, model_width)
    token_part = jnp.dot(chosen.T, expert_in, precision=lax.Precision.HIGHEST)
    token_sum = lax.psum(token_part, "expert")
    return (
        mixed_sum.astype(jnp.bfloat16),
        route_sum,
        token_sum.astype(jnp.bfloat16),
        grad_gate[None],
        grad_up[None],
        grad_down[None],
    )


def solution(mesh):
    in_specs = (
        P("dp", None),
        P("dp", None),
        P(),
        P(),
        P(("expert", "dp"), None, None),
        P(("expert", "dp"), None, None),
        P(("expert", "dp"), None, None),
    )
    out_specs = (
        P("dp", None),
        P("dp", None),
        P("dp", None),
        P(("expert", "dp"), None, None),
        P(("expert", "dp"), None, None),
        P(("expert", "dp"), None, None),
    )
    return jax.shard_map(body, mesh=mesh, in_specs=in_specs, out_specs=out_specs, check_vma=False)
```

profile of v0, /device:TPU:0, one launch (start us, length us, event | category | flops | bytes accessed | tf_op | source)
XLA Modules:
  0.0 185.1 jit_solution(8156129341371155405)
XLA Ops:
  7.2 0.0 copy-start
  7.2 0.0 all-gather.3.cloned.1.call-start
  7.2 0.7 all-gather.3.cloned.1.call-update
  7.9 0.0 all-gather.5.cloned.1.call-start
  8.0 0.7 all-gather.5.cloned.1.call-update
  8.7 0.8 reshape.134
  9.4 0.8 copy.39
  10.3 0.1 eq.82
  10.4 0.9 reduce-window.14
  11.3 0.2 slice_reduce_fusion
  11.6 0.1 eq.89
  11.7 0.1 eq.93
  11.9 0.1 eq.78
  12.0 0.1 fusion.35
  12.1 0.1 reduce_sum.90
  12.3 0.1 copy.41
  12.4 3.4 %reduce-window.16 = s32[4,16,3,128]{3,1,2,0:T(8,128)S(1)} reduce-window(s32[4,16,3,128]{3,1,2,0:T(8,128)S(1)} %fusion.29, s32[]{:T(128)} %constant.47.clone.1), window={size=1x1x1x128 pad=0_0x0_0x0_0x127_0}, to_apply=%region_4.5 | reduce-window | flops 3121152 | bytes 196612 | tf_op jit(solution)/shard_map/reduce-window.2
  15.8 0.1 slice.17
  15.9 0.1 copy.44
  16.1 0.1 fusion.28
  16.2 0.1 reduce_sum.93
  16.4 0.1 copy.47
  16.5 0.3 select_reduce_fusion
  16.8 22.4 %all-gather.3.cloned.1.call-done = bf16[256,2048]{1,0:T(8,128)(2,1)} async-done(((bf16[64,2048]{1,0:T(8,128)(2,1)}), bf16[256,2048]{1,0:T(8,128)(2,1)}) %all-gather.3.cloned.1.call-update) | async-done | bytes 1048592 | tf_op jit(solution)/shard_map/all_gather | solution.py:66
  39.2 2.6 %convolution_convert_fusion.3 = bf16[4,64,2048]{2,1,0:T(8,128)(2,1)} fusion(bf16[4,64,2048]{2,1,0:T(8,128)(2,1)} %bitcast.129, bf16[4,64,64]{2,1,0:T(8,128)(2,1)S(1)} %get-tuple-element.7), kind=kOutput, calls=%fused_computation.23 | convolution fusion | flops 67633152 | bytes 2129920 | tf_op jit(solution)/shard_map/sct,std->scd/dot_general | solution.py:80
  41.8 25.9 %all-gather.5.cloned.1.call-done = bf16[256,2048]{1,0:T(8,128)(2,1)} async-done(((bf16[64,2048]{1,0:T(8,128)(2,1)}), bf16[256,2048]{1,0:T(8,128)(2,1)}) %all-gather.5.cloned.1.call-update) | async-done | bytes 1048592 | tf_op jit(solution)/shard_map/all_gather | solution.py:67
  67.7 1.6 fusion.21
  69.4 0.0 copy-start.1
  69.4 0.0 copy-start.3
  69.4 2.9 %fusion.3 = f32[256,704]{0,1:T(8,128)S(1)} fusion(bf16[256,2048]{1,0:T(8,128)(2,1)S(1)} %bitcast.127, bf16[1,704,2048]{2,1,0:T(8,128)(2,1)} %param.13), kind=kOutput, calls=%fused_computation.6 | convolution fusion | flops 738197504 | bytes 4653056 | tf_op jit(solution)/shard_map/dot_general | solution.py:40
  72.3 0.0 copy-done.1
  72.3 0.0 copy-done.3
  72.3 1.0 fusion.9
  73.4 0.0 copy-done
  73.4 0.0 copy-start.7
  73.4 1.9 %multiply_convert_fusion.1 = (bf16[256,704]{0,1:T(8,128)(2,1)S(1)}, bf16[256,704]{0,1:T(8,128)(2,1)}, bf16[256,704]{0,1:T(8,128)(2,1)S(1)}) fusion(f32[256,704]{0,1:T(8,128)S(1)} %fusion.3, f32[256,704]{0,1:T(8,128)S(1)} %fusion.9, bf16[256,2048]{1,0:T(8,128)(2,1)S(1)} %bitcast.132, bf16[1,704,2048]{2,1,0:T(8,128)(2,1)S(1)} %copy-done), kind=kOutput, calls=%fused_computation.30 | convolution fusion | flops 740900864 | bytes 6455296 | tf_op jit(solution)/shard_map/dot_general | solution.py:40
  75.3 0.0 copy-done.7
  75.3 2.0 %fusion.22 = bf16[256,2048]{1,0:T(8,128)(2,1)} fusion(bf16[256,704]{0,1:T(8,128)(2,1)S(1)} %get-tuple-element.16, bf16[1,704,2048]{2,1,0:T(8,128)(2,1)S(1)} %copy-done.7), kind=kOutput, calls=%fused_computation.22 | convolution fusion | flops 738721792 | bytes 4292608 | tf_op jit(solution)/shard_map/dot_general | solution.py:96
  77.4 2.5 %fusion.2 = bf16[1,704,2048]{2,1,0:T(8,128)(2,1)} fusion(bf16[256,704]{0,1:T(8,128)(2,1)S(1)} %get-tuple-element.16, bf16[256,2048]{1,0:T(8,128)(2,1)S(1)} %bitcast.128), kind=kOutput, calls=%fused_computation.5 | convolution fusion | flops 739639296 | bytes 4292608 | tf_op jit(solution)/shard_map/dot_general | solution.py:34
  79.9 4.2 %all-to-all-start = ((bf16[4,64,2048]{2,1,0:T(8,128)(2,1)}), bf16[4,64,2048]{2,1,0:T(8,128)(2,1)}, u32[]{:S(2)}, u32[]{:S(2)}) async-start(bf16[4,64,2048]{2,1,0:T(8,128)(2,1)} %bitcast.134), calls=%async_computation | async-start | bytes 2097152 | tf_op jit(solution)/shard_map/all_to_all | solution.py:97
  84.1 0.0 copy-start.4
  84.1 0.0 copy-start.6
  84.1 3.8 %fusion = bf16[1,704,2048]{2,1,0:T(8,128)(2,1)} fusion(bf16[256,704]{0,1:T(8,128)(2,1)S(1)} %get-tuple-element.14, bf16[256,2048]{1,0:T(8,128)(2,1)} %bitcast.130), kind=kOutput, calls=%fused_computation.3 | convolution fusion | flops 739639296 | bytes 4292608 | tf_op jit(solution)/shard_map/dot_general | solution.py:34
  87.9 0.0 copy-start.2
  87.9 0.0 copy-done.4
  87.9 0.0 copy-done.6
  88.0 2.5 %fusion.1 = bf16[1,704,2048]{2,1,0:T(8,128)(2,1)} fusion(bf16[256,704]{0,1:T(8,128)(2,1)S(1)} %copy-done.6, bf16[256,2048]{1,0:T(8,128)(2,1)S(1)} %bitcast.133), kind=kOutput, calls=%fused_computation.4 | convolution fusion | flops 739639296 | bytes 4292608 | tf_op jit(solution)/shard_map/dot_general | solution.py:34
  90.4 0.0 copy-done.2
  90.5 1.0 fusion.7
  91.4 2.0 %fusion.18 = bf16[256,2048]{1,0:T(8,128)(2,1)} fusion(f32[256,2048]{1,0:T(8,128)S(1)} %fusion.7, bf16[256,704]{0,1:T(8,128)(2,1)S(1)} %get-tuple-element.14, bf16[1,704,2048]{2,1,0:T(8,128)(2,1)S(1)} %copy-done), kind=kOutput, calls=%fused_computation.20 | convolution fusion | flops 739246080 | bytes 6389760 | tf_op jit(solution)/shard_map/dot_general | solution.py:121
  93.4 0.0 copy-start.5
  93.5 4.6 %all-to-all-done = bf16[4,64,2048]{2,1,0:T(8,128)(2,1)} async-done(((bf16[4,64,2048]{2,1,0:T(8,128)(2,1)}), bf16[4,64,2048]{2,1,0:T(8,128)(2,1)}, u32[]{:S(2)}, u32[]{:S(2)}) %all-to-all-start) | async-done | bytes 1048608 | tf_op jit(solution)/shard_map/all_to_all | solution.py:97
  98.1 4.4 %all-to-all-start.1 = ((bf16[4,64,2048]{2,1,0:T(8,128)(2,1)}), bf16[4,64,2048]{2,1,0:T(8,128)(2,1)}, u32[]{:S(2)}, u32[]{:S(2)}) async-start(bf16[4,64,2048]{2,1,0:T(8,128)(2,1)} %bitcast.121), calls=%async_computation.1 | async-start | bytes 2097152 | tf_op jit(solution)/shard_map/all_to_all | solution.py:124
  102.5 1.5 convert_reduce_fusion.1
  104.0 0.0 copy-done.5
  104.0 0.7 fusion.40
  104.8 0.3 convert_reduce_fusion.3
  105.0 0.7 fusion.39
  105.7 9.8 %all-to-all-done.1 = bf16[4,64,2048]{2,1,0:T(8,128)(2,1)} async-done(((bf16[4,64,2048]{2,1,0:T(8,128)(2,1)}), bf16[4,64,2048]{2,1,0:T(8,128)(2,1)}, u32[]{:S(2)}, u32[]{:S(2)}) %all-to-all-start.1) | async-done | bytes 1048608 | tf_op jit(solution)/shard_map/all_to_all | solution.py:124
  115.5 1.5 convert_reduce_fusion
  117.0 1.5 fusion.41
  118.5 59.8 %all-reduce.2 = (bf16[64,2048]{1,0:T(8,128)(2,1)}, f32[64,6]{0,1:T(8,128)}, bf16[64,2048]{1,0:T(8,128)(2,1)}) all-reduce(f32[64,2048]{1,0:T(8,128)S(1)} %fusion.39, f32[64,6]{0,1:T(8,128)S(1)} %get-tuple-element.9, f32[64,2048]{1,0:T(8,128)} %fusion.41), channel_id=1, replica_groups=mesh['dp'=4,'expert'=8] {'expert'}, use_global_device_ids=true, to_apply=%region_9.10 | all-reduce | flops 262528 | bytes 1575936 | tf_op jit(solution)/shard_map/psum | solution.py:111
  (12 shorter events, 0.2 us)
Async XLA Ops:
  7.2 66.2 %copy-start = (bf16[1,704,2048]{2,1,0:T(8,128)(2,1)S(1)}, bf16[1,704,2048]{2,1,0:T(8,128)(2,1)}, u32[]{:S(2)}) copy-start(bf16[1,704,2048]{2,1,0:T(8,128)(2,1)} %param.11) | copy-start | bytes 8650756
  7.2 32.0 %all-gather.3.cloned.1.call-start = ((), (), s32[]{:S(2)}) async-start(), calls=%async_computation.2 | async-start | bytes 1310720 | tf_op jit(solution)/shard_map/all_gather | solution.py:66
  7.9 59.8 %all-gather.5.cloned.1.call-start = ((), (), s32[]{:S(2)}) async-start(), calls=%async_computation.3 | async-start | bytes 1310720 | tf_op jit(solution)/shard_map/all_gather | solution.py:67
  69.4 2.9 %copy-start.1 = (bf16[1,704,2048]{2,1,0:T(8,128)(2,1)S(1)}, bf16[1,704,2048]{2,1,0:T(8,128)(2,1)}, u32[]{:S(2)}) copy-start(bf16[1,704,2048]{2,1,0:T(8,128)(2,1)} %param.12) | copy-start | bytes 8650756
  69.4 2.9 %copy-start.3 = (bf16[4,64,2048]{2,1,0:T(8,128)(2,1)S(1)}, bf16[4,64,2048]{2,1,0:T(8,128)(2,1)}, u32[]{:S(2)}) copy-start(bf16[4,64,2048]{2,1,0:T(8,128)(2,1)} %convolution_convert_fusion.3) | copy-start | bytes 3145732
  73.4 2.0 %copy-start.7 = (bf16[1,704,2048]{2,1,0:T(8,128)(2,1)S(1)}, bf16[1,704,2048]{2,1,0:T(8,128)(2,1)}, u32[]{:S(2)}) copy-start(bf16[1,704,2048]{2,1,0:T(8,128)(2,1)} %param.13) | copy-start | bytes 8650756
  79.9 18.2 %all-to-all-start = ((bf16[4,64,2048]{2,1,0:T(8,128)(2,1)}), bf16[4,64,2048]{2,1,0:T(8,128)(2,1)}, u32[]{:S(2)}, u32[]{:S(2)}) async-start(bf16[4,64,2048]{2,1,0:T(8,128)(2,1)} %bitcast.134), calls=%async_computation | async-start | bytes 2097152 | tf_op jit(solution)/shard_map/all_to_all | solution.py:97
  84.1 3.9 %copy-start.4 = (bf16[4,64,2048]{2,1,0:T(8,128)(2,1)S(1)}, bf16[4,64,2048]{2,1,0:T(8,128)(2,1)}, u32[]{:S(2)}) copy-start(bf16[4,64,2048]{2,1,0:T(8,128)(2,1)} %convolution_convert_fusion.3) | copy-start | bytes 3145732
  84.1 3.8 %copy-start.6 = (bf16[256,704]{0,1:T(8,128)(2,1)S(1)}, bf16[256,704]{0,1:T(8,128)(2,1)}, u32[]{:S(2)}) copy-start(bf16[256,704]{0,1:T(8,128)(2,1)} %get-tuple-element.15) | copy-start | bytes 1081348
  87.9 2.5 %copy-start.2 = (bf16[1,704,2048]{2,1,0:T(8,128)(2,1)S(1)}, bf16[1,704,2048]{2,1,0:T(8,128)(2,1)}, u32[]{:S(2)}) copy-start(bf16[1,704,2048]{2,1,0:T(8,128)(2,1)} %param.12) | copy-start | bytes 8650756
  93.4 10.6 %copy-start.5 = (bf16[64,2048]{1,0:T(8,128)(2,1)S(1)}, bf16[64,2048]{1,0:T(8,128)(2,1)}, u32[]{:S(2)}) copy-start(bf16[64,2048]{1,0:T(8,128)(2,1)} %param.8) | copy-start | bytes 786436
  98.1 17.5 %all-to-all-start.1 = ((bf16[4,64,2048]{2,1,0:T(8,128)(2,1)}), bf16[4,64,2048]{2,1,0:T(8,128)(2,1)}, u32[]{:S(2)}, u32[]{:S(2)}) async-start(bf16[4,64,2048]{2,1,0:T(8,128)(2,1)} %bitcast.121), calls=%async_computation.1 | async-start | bytes 2097152 | tf_op jit(solution)/shard_map/all_to_all | solution.py:124
Sparse Core Ops, SparseCore 0:
  9.9 29.3 all-gather.2
  41.1 26.6 all-gather.4
where the time goes:
time: 186 us; the launch traced here: 185 us
  waiting for transfers between devices  64.1 us (34%)
  blocking collectives  59.8 us (32%)
  matrix products  26.9 us (14%)
  between operations  14.3 us (8%)
  starting transfers between devices  8.75 us (5%)
  other arithmetic  8.19 us (4%)
  local copies, waits for them, and re-layouts  3.15 us (2%)
    psum x1, blocking collectives, body(): mixed_sum, route_sum = lax.psum((mixed_part, route_part), 'expert')  59.8 us
    all_gather x1, waiting for transfers between devices, body(): lax.all_gather(d_mixed, 'dp', axis=0, tiled=True)  25.9 us
    all_gather x1, waiting for transfers between devices, body(): lax.all_gather(tokens, 'dp', axis=0, tiled=True)  22.4 us
    all_to_all x1, waiting for transfers between devices, body(): lax.all_to_all(part_in.reshape(dp_count, capacity, model_width), 'dp', sp...  9.79 us
    dot_general x3, matrix products, contract_first(): lax.dot_general(left, right, (((0,), (0,)), ((), ())), preferred_element_...  8.82 us
    dot_general x3, matrix products, contract_last(): lax.dot_general(left, right, (((1,), (1,)), ((), ())), preferred_element_...  5.87 us
    all_to_all x1, waiting for transfers between devices, body(): lax.all_to_all(part_out.reshape(dp_count, capacity, model_width), 'dp', s...  4.62 us
    all_to_all x1, starting transfers between devices, body(): lax.all_to_all(part_in.reshape(dp_count, capacity, model_width), 'dp', sp...  4.44 us
  transfers between devices with their start and end apart: 4, of which 4 were waited for; matrix products, arithmetic and copies ran while one was open for 12% of the time, Pallas kernels for 0%

commit v1 on v0

v1 whole, which is shorter than its diff:
```python
import functools
import math

import jax
import jax.numpy as jnp
from jax import lax
from jax.experimental import pallas as pl
from jax.experimental.pallas import tpu as pltpu
from jax.sharding import PartitionSpec as P

EXP_DEV = 2
CORES = 2
MESH = pl.DeviceIdType.MESH
F32 = jnp.float32
BF16 = jnp.bfloat16


def dot(left, right, lhs_dim, rhs_dim):
    return lax.dot_general(
        left, right, (((lhs_dim,), (rhs_dim,)), ((), ())), preferred_element_type=F32
    )


def kernel(
    shape, tok, dmx, ids, wts, gate_hbm, up_hbm, down_hbm,
    mixed_out, route_out, dtok_out, ggate_out, gup_out, gdown_out,
    xs, ds, wg, wu, wd, gate, up, dhid, hw, dg, du,
    ps0, ps1, pr0, pr1, acc0, acc1, sb0, sb1, ra0, ra1, sc0, sc1, rb0, rb1,
    zb0, zb1, zf0, zf1, rz0, rz1, ag0, ag1, stage,
    send_sem, recv_sem, load_sem, store_sem,
):
    n_dp, side, n_z, rows, half, hid, row_parts, tile = shape
    ps, pr, acc, sb, ra = (ps0, ps1), (pr0, pr1), (acc0, acc1), (sb0, sb1), (ra0, ra1)
    sc, rb, zb, zf, rz, ag = (sc0, sc1), (rb0, rb1), (zb0, zb1), (zf0, zf1), (rz0, rz1), (ag0, ag1)
    dp = lax.axis_index("dp")
    column = lax.axis_index("expert")
    core = lax.rem(column, CORES)
    z = column // CORES
    step_a = 1 + core * (side - 1)
    step_b = side - core * (side - 1)
    a = lax.rem(dp // step_a, side)
    b = lax.rem(dp // step_b, side)

    def block_of(a_index, b_index):
        return a_index * step_a + b_index * step_b

    def turn(value, by, size):
        return lax.rem(value + by + size, size)

    sibling = (dp, column + 1 - 2 * core)

    def peer_a(by):
        return (block_of(turn(a, by, side), b), column)

    def peer_b(by):
        return (block_of(a, turn(b, by, side)), column)

    def peer_z(by):
        return (dp, turn(z, by, n_z) * CORES + core)

    partners = [sibling]
    partners += [peer_a(k) for k in range(1, side)]
    partners += [peer_b(k) for k in range(1, side)]
    partners += [peer_z(k) for k in range(1, n_z)]

    loads = []
    for number, (source, target) in enumerate(((gate_hbm, wg), (up_hbm, wu), (down_hbm, wd))):
        loads.append(pltpu.make_async_copy(source.at[0], target, load_sem.at[number]))
        loads[-1].start()

    used = [0]
    sent = []

    def send(source, target, device):
        copy = pltpu.make_async_remote_copy(
            src_ref=source, dst_ref=target, send_sem=send_sem.at[used[0]],
            recv_sem=recv_sem.at[used[0]], device_id=device, device_id_type=MESH,
        )
        used[0] += 1
        copy.start()
        sent.append(copy)
        return copy

    barrier = pltpu.get_barrier_semaphore()
    for partner in partners:
        pl.semaphore_signal(barrier, inc=1, device_id=partner, device_id_type=MESH)
    for part in range(CORES):
        xs[part, dp] = tok[:, part * half : (part + 1) * half]
        ds[part, dp] = dmx[:, part * half : (part + 1) * half]
    pl.semaphore_wait(barrier, len(partners))

    from_a, from_b, from_ab, from_core = [], [], [], []
    for buffer in (xs, ds):
        own = buffer.at[core, dp]
        from_a.append([send(own, own, peer_a(k)) for k in range(1, side)])
        from_b.append([send(own, own, peer_b(k)) for k in range(1, side)])
    for number, buffer in enumerate((xs, ds)):
        from_ab.append([])
        from_core.append([])
        for k in range(1, side):
            from_a[number][k - 1].wait_recv()
            got = buffer.at[core, block_of(turn(a, -k, side), b)]
            for m in range(1, side):
                from_ab[number].append(send(got, got, peer_b(m)))
            from_core[number].append(send(got, got, sibling))

    def finish_gather(number, buffer):
        for k in range(1, side):
            from_b[number][k - 1].wait_recv()
            got = buffer.at[core, block_of(a, turn(b, -k, side))]
            from_core[number].append(send(got, got, sibling))
        for k in range(1, side):
            for m in range(1, side):
                from_ab[number][(k - 1) * (side - 1) + m - 1].wait_recv()
                got = buffer.at[core, block_of(turn(a, -k, side), turn(b, -m, side))]
                from_core[number].append(send(got, got, sibling))

    def whole(buffer, part):
        return buffer[part].reshape(n_dp * rows, half)

    finish_gather(0, xs)
    for copy in from_core[0]:
        copy.wait_recv()
    loads[0].wait()
    gate[...] = dot(whole(xs, 0), wg[:, :half], 1, 1) + dot(whole(xs, 1), wg[:, half:], 1, 1)
    finish_gather(1, ds)
    loads[1].wait()
    up[...] = dot(whole(xs, 0), wu[:, :half], 1, 1) + dot(whole(xs, 1), wu[:, half:], 1, 1)
    for copy in from_core[1]:
        copy.wait_recv()
    loads[2].wait()
    dhid[...] = dot(whole(ds, 0), wd[:, :half], 1, 1) + dot(whole(ds, 1), wd[:, half:], 1, 1)

    pieces = n_dp // EXP_DEV
    expert = column * EXP_DEV + dp // pieces
    piece = lax.rem(dp, pieces)
    strip = rows // 2

    @pl.loop(0, 2 * n_dp)
    def elementwise(index):
        start = pl.multiple_of(index * strip, strip)
        span = pl.ds(start, strip)
        lane = lax.broadcasted_iota(jnp.int32, (strip, 128), 1)
        named = ids[span, :] == expert
        weight = jnp.sum(jnp.where(named & (lane < 8), wts[span, :], 0.0), axis=1, keepdims=True)
        gate_value = gate[span, :]
        up_value = up[span, :]
        plain = dhid[span, :]
        sigmoid_gate = 1.0 / (1.0 + jnp.exp(-gate_value))
        activated = gate_value * sigmoid_gate
        hidden = activated * up_value
        paired = jnp.sum(hidden * plain, axis=1, keepdims=True)
        d_hidden = weight * plain
        hw[span, :] = (weight * hidden).astype(BF16)
        dg[span, :] = (
            d_hidden * up_value * sigmoid_gate * (1.0 + gate_value * (1.0 - sigmoid_gate))
        ).astype(BF16)
        du[span, :] = (d_hidden * activated).astype(BF16)
        leading = paired.astype(BF16).astype(F32)
        share = jnp.where(lane < 64, leading, paired - leading)
        mine = named & (lax.rem(lane // 8, 8) == piece)
        block = index // 2
        inner = pl.ds(pl.multiple_of(lax.rem(index, 2) * strip, strip), strip)
        acc0[block, inner, half : half + 128] = jnp.where(mine, share, 0.0)
        if acc0.shape[2] > half + 128:
            acc0[block, inner, half + 128 :] = jnp.zeros(
                (strip, acc0.shape[2] - half - 128), F32
            )

    def product(which, columns):
        if which == 0:
            return dot(hw[...], wd[:, columns], 1, 0)
        return dot(dg[...], wg[:, columns], 1, 0) + dot(du[...], wu[:, columns], 1, 0)

    pair = []
    for q in range(2):

        @pl.loop(0, half // tile)
        def other_half(t, q=q):
            start = pl.multiple_of((1 - core) * half + t * tile, tile)
            value = product(q, pl.ds(start, tile)).astype(BF16)
            ps[q][:, :, pl.ds(pl.multiple_of(t * tile, tile), tile)] = value.reshape(
                n_dp, rows, tile
            )

        pair.append(send(ps[q], pr[q], sibling))

        @pl.loop(0, half // tile)
        def own_half(t, q=q):
            start = pl.multiple_of(core * half + t * tile, tile)
            value = product(q, pl.ds(start, tile))
            acc[q][:, :, pl.ds(pl.multiple_of(t * tile, tile), tile)] = value.reshape(
                n_dp, rows, tile
            )

    stores = []

    def weight_grad(number, left, buffer, target):
        for part in range(CORES):

            @pl.loop(0, half // tile)
            def columns(t, part=part):
                inner = pl.ds(pl.multiple_of(t * tile, tile), tile)
                right = buffer[part, :, :, inner].reshape(n_dp * rows, tile)
                start = pl.multiple_of(part * half + t * tile, tile)
                stage[number, :, pl.ds(start, tile)] = dot(left[...], right, 0, 0).astype(BF16)

        stores.append(pltpu.make_async_copy(stage.at[number], target.at[0], store_sem.at[number]))
        stores[-1].start()

    def pair_done(q):
        pair[q].wait_recv()

        @pl.loop(0, n_dp)
        def add(block):
            total = acc[q][block, :, :half] + pr[q][block].astype(F32)
            acc[q][block, :, :half] = total
            sb[q][block, :, :half] = total.astype(BF16)
            if acc[q].shape[2] > half:
                sb[q][block, :, half:] = acc[q][block, :, half:].astype(BF16)

        copies = []
        for k in range(1, side):
            for m in range(side):
                source = sb[q].at[block_of(turn(a, k, side), m)]
                copies.append(send(source, ra[q].at[k - 1, m], peer_a(k)))
        return copies

    def first_done(q, copies):
        for copy in copies:
            copy.wait_recv()
        following = []
        for m in range(1, side + 1):
            goal = turn(b, m, side)
            total = acc[q][block_of(a, goal)]
            for k in range(1, side):
                total = total + ra[q][k - 1, goal].astype(F32)
            if m < side:
                sc[q][m - 1] = total.astype(BF16)
                following.append(send(sc[q].at[m - 1], rb[q].at[m - 1], peer_b(m)))
            else:
                acc[q][block_of(a, b)] = total
        return following

    def second_done(q, copies):
        for copy in copies:
            copy.wait_recv()
        total = acc[q][block_of(a, b)]
        for k in range(1, side):
            total = total + rb[q][k - 1].astype(F32)
        high, wide = zb[q].shape[1:]
        for part in range(n_z):
            top = (part % row_parts) * high
            left = (part // row_parts) * wide
            value = total[top : top + high, left : left + wide]
            zf[q][part] = value
            zb[q][part] = value.astype(BF16)
        return [
            send(zb[q].at[turn(z, k, n_z)], rz[q].at[k - 1], peer_z(k)) for k in range(1, n_z)
        ]

    def third_done(q, copies):
        for copy in copies:
            copy.wait_recv()
        total = zf[q][z]
        for k in range(1, n_z):
            total = total + rz[q][k - 1].astype(F32)
        ag[q][core, z] = total.astype(BF16)
        own = ag[q].at[core, z]
        following = [send(own, own, peer_z(k)) for k in range(1, n_z)]
        return following, [send(own, own, sibling)]

    def fourth_done(q, copies, shared):
        for k in range(1, n_z):
            copies[k - 1].wait_recv()
            got = ag[q].at[core, turn(z, -k, n_z)]
            shared.append(send(got, got, sibling))

    first0 = pair_done(0)
    first1 = pair_done(1)
    weight_grad(0, hw, ds, gdown_out)
    second0 = first_done(0, first0)
    weight_grad(1, dg, xs, ggate_out)
    second1 = first_done(1, first1)
    third0 = second_done(0, second0)
    weight_grad(2, du, xs, gup_out)
    third1 = second_done(1, second1)
    fourth0, shared0 = third_done(0, third0)
    fourth1, shared1 = third_done(1, third1)
    fourth_done(0, fourth0, shared0)
    fourth_done(1, fourth1, shared1)

    for q, (target, shared) in enumerate(((mixed_out, shared0), (dtok_out, shared1))):
        for copy in shared:
            copy.wait_recv()
        high, wide = zb[q].shape[1:]
        routes = []
        for part in range(row_parts):
            span = slice(part * high, (part + 1) * high)
            for side_core in range(CORES):
                strips = [ag[q][side_core, k * row_parts + part] for k in range(n_z // row_parts)]
                line = strips[0] if len(strips) == 1 else jnp.concatenate(strips, axis=1)
                target[span, side_core * half : (side_core + 1) * half] = line[:, :half]
                if q == 0:
                    routes.append(line[:, half : half + 128].astype(F32))
            if q == 0:
                total = routes[-2] + routes[-1]
                for by in (64, 32, 16, 8):
                    total = total + pltpu.roll(total, by, 1)
                route_out[span, :] = total
    for copy in sent:
        copy.wait_send()
    for copy in stores:
        copy.wait()


def body(tokens, d_mixed, route_ids, route_weight, gate_weight, up_weight, down_weight):
    n_dp = lax.axis_size("dp")
    n_z = lax.axis_size("expert") // CORES
    side = math.isqrt(n_dp)
    rows, width = tokens.shape
    choices = route_ids.shape[1]
    hid = gate_weight.shape[1]
    half = width // CORES
    tile = 256
    row_parts = min(n_z, rows // 16)
    col_parts = n_z // row_parts
    high = rows // row_parts
    pad = ((0, 0), (0, 8 - choices))
    ids = jnp.tile(jnp.pad(route_ids, pad, constant_values=-1), (1, 16))
    wts = jnp.tile(jnp.pad(route_weight, pad), (1, 16))
    widths = (half + 128 * col_parts, half)
    total_rows = n_dp * rows

    def both(make):
        return [make(w) for w in widths]

    def vmem(*dims, dtype=BF16):
        return pltpu.VMEM(dims, dtype)

    scratch = [vmem(CORES, n_dp, rows, half)] * 2
    scratch += [vmem(hid, width)] * 3
    scratch += [vmem(total_rows, hid, dtype=F32)] * 3
    scratch += [vmem(total_rows, hid)] * 3
    scratch += [vmem(n_dp, rows, half)] * 4
    scratch += both(lambda w: vmem(n_dp, rows, w, dtype=F32))
    scratch += both(lambda w: vmem(n_dp, rows, w))
    scratch += both(lambda w: vmem(side - 1, side, rows, w))
    scratch += both(lambda w: vmem(side - 1, rows, w))
    scratch += both(lambda w: vmem(side - 1, rows, w))
    scratch += both(lambda w: vmem(n_z, high, w // col_parts))
    scratch += both(lambda w: vmem(n_z, high, w // col_parts, dtype=F32))
    scratch += both(lambda w: vmem(n_z - 1, high, w // col_parts))
    scratch += both(lambda w: vmem(CORES, n_z, high, w // col_parts))
    scratch += [vmem(3, hid, width)]
    gather = 2 * (2 * (side - 1) + (side - 1) ** 2 + n_dp - 1)
    reduce = 2 * (1 + (side - 1) * side + side - 1 + 2 * (n_z - 1) + n_z)
    copies = gather + reduce
    scratch += [pltpu.SemaphoreType.DMA((copies,))] * 2 + [pltpu.SemaphoreType.DMA((3,))] * 2

    in_vmem = pl.BlockSpec(memory_space=pltpu.VMEM)
    anywhere = pl.BlockSpec(memory_space=pl.ANY)
    grad = jax.ShapeDtypeStruct((1, hid, width), BF16)
    flat = jax.ShapeDtypeStruct((rows, width), BF16)
    shape = (n_dp, side, n_z, rows, half, hid, row_parts, tile)
    mixed, route, d_tokens, grad_gate, grad_up, grad_down = pl.pallas_call(
        functools.partial(kernel, shape),
        out_shape=(flat, jax.ShapeDtypeStruct((rows, 128), F32), flat, grad, grad, grad),
        in_specs=[in_vmem] * 4 + [anywhere] * 3,
        out_specs=(in_vmem,) * 3 + (anywhere,) * 3,
        scratch_shapes=scratch,
        compiler_params=pltpu.CompilerParams(
            collective_id=0, has_side_effects=True, vmem_limit_bytes=60 * 1024 * 1024
        ),
        cost_estimate=pl.CostEstimate(
            flops=18 * total_rows * hid * width,
            bytes_accessed=12 * hid * width,
            transcendentals=total_rows * hid,
        ),
    )(tokens, d_mixed, ids, wts, gate_weight, up_weight, down_weight)
    return mixed, route[:, :choices], d_tokens, grad_gate, grad_up, grad_down


def solution(mesh):
    row, whole, block = P("dp", None), P(), P(("expert", "dp"), None, None)
    return jax.shard_map(
        body,
        mesh=mesh,
        in_specs=(row, row, whole, whole, block, block, block),
        out_specs=(row, row, row, block, block, block),
        check_vma=False,
    )
```

time: 186 us -> 70.6 us (0.38)
  waiting for transfers between devices: 64.1 us -> 0 us
  blocking collectives: 59.8 us -> 0 us
  Pallas kernels: 0 us -> 53.5 us
  matrix products: 26.9 us -> 0 us
  between operations: 14.3 us -> 0.65 us
  local copies, waits for them, and re-layouts: 3.15 us -> 16 us
  starting transfers between devices: 8.75 us -> 0 us
  other arithmetic: 8.19 us -> 0 us
    psum x1 -> x0, blocking collectives: 59.8 us -> none  [body(): mixed_sum, route_sum = lax.psum((mixed_part, route_part), 'expert')]
    pallas_call x0 -> x1, Pallas kernels: none -> 53.5 us  [body(): pl.pallas_call(functools.partial(kernel, shape), out_shape=(flat, jax.Sha...]
    all_gather x2 -> x0, waiting for transfers between devices: 48.3 us -> none  [the longest x1 25.9 us: body(): lax.all_gather(d_mixed, 'dp', axis=0, tiled=True)]
    dot_general x14 -> x0, matrix products: 26.9 us -> none  [the longest x3 8.82 us: contract_first(): lax.dot_general(left, right, (((0,), (0,)), ((), ())), preferred_element_...]
    all_to_all x2 -> x0, waiting for transfers between devices: 14.4 us -> none  [the longest x1 9.79 us: body(): lax.all_to_all(part_in.reshape(dp_count, capacity, model_width), 'dp', sp...]
    unnamed x18 -> x10, local copies, waits for them, and re-layouts: 0.88 us -> 13.1 us
    all_to_all x2 -> x0, starting transfers between devices: 8.68 us -> none  [the longest x1 4.44 us: body(): lax.all_to_all(part_in.reshape(dp_count, capacity, model_width), 'dp', sp...]
    another operation x4 -> x0, other arithmetic: 4.34 us -> none
  transfers between devices with their start and end apart: 4 -> 0, of which waited for: 4 -> 0; matrix products, arithmetic and copies ran while one was open for 12% -> 0% of each run, Pallas kernels for 0% -> 0%
where the time goes in v1:
time: 70.6 us; the launch traced here: 70.2 us
  Pallas kernels  53.5 us (76%)
  local copies, waits for them, and re-layouts  16 us (23%)
    pallas_call x1, Pallas kernels, body(): pl.pallas_call(functools.partial(kernel, shape), out_shape=(flat, jax.Sha...  53.5 us
    unnamed x10, local copies, waits for them, and re-layouts  13.1 us

profile of v1, /device:TPU:0, one launch (start us, length us, event | category | flops | bytes accessed | tf_op | source)
XLA Modules:
  0.0 70.2 jit_solution(2548307438194500109)
XLA Ops:
  0.6 0.7 %pad.8 = s32[256,8]{0,1:T(8,128)S(1)} pad(s32[256,6]{0,1:T(8,128)} %param.9, s32[]{:T(128)} %constant.1.clone.1), padding=0_0x0_2 | pad | bytes 14340 | tf_op jit(solution)/shard_map/jit(_pad)/pad | solution.py:330
  1.3 0.7 pad.9
  2.0 0.8 %copy.17.wts = f32[256,128]{1,0:T(8,128)} copy(f32[256,128]{0,1:T(8,128)S(1)} %broadcast_bitcast_fusion) | data formatting | bytes 262144 | tf_op jit(solution)/shard_map/tile | solution.py:331
  2.8 0.8 %copy.16.ids = s32[256,128]{1,0:T(8,128)} copy(s32[256,128]{0,1:T(8,128)S(1)} %broadcast_bitcast_fusion.1) | data formatting | bytes 262144 | tf_op jit(solution)/shard_map/tile | solution.py:330
  3.6 53.5 %shard_map.118 = (bf16[64,2048]{1,0:T(8,128)(2,1)}, f32[64,128]{1,0:T(8,128)}, bf16[64,2048]{1,0:T(8,128)(2,1)}, bf16[1,704,2048]{2,1,0:T(8,128)(2,1)}, bf16[1,7...) custom-call(bf16[64,2048]{1,0:T(8,128)(2,1)} %tok.1, bf16[64,2048]{1,0:T(8,128)(2,1)} %dmx.1, s32[256,128]{1,0:T(8,128)} %copy.16.ids, ...), custom_call_target="tpu_custom_call" | custom-call | flops 6643777536 | bytes 17301504 | tf_op jit(solution)/shard_map/pallas_call | solution.py:366
  57.1 1.4 %copy.18 = f32[64,6]{0,1:T(8,128)} copy(f32[64,6]{1,0:T(8,128)} %bitcast.5) | data formatting | bytes 3072
  58.5 1.7 %copy.24 = bf16[64,2048]{1,0:T(8,128)(2,1)} copy(bf16[64,2048]{1,0:T(8,128)(2,1)} %get-tuple-element.36) | data formatting | bytes 524288
  60.2 1.7 %copy.25 = bf16[64,2048]{1,0:T(8,128)(2,1)} copy(bf16[64,2048]{1,0:T(8,128)(2,1)} %get-tuple-element.38) | data formatting | bytes 524288
  61.9 0.0 copy-start.1
  61.9 3.9 %copy.26 = bf16[1,704,2048]{2,1,0:T(8,128)(2,1)} copy(bf16[1,704,2048]{2,1,0:T(8,128)(2,1)} %get-tuple-element.39) | data formatting | bytes 5767168
  65.8 0.0 copy-done.1
  65.8 0.0 copy-start
  65.8 1.6 %copy.27 = bf16[1,704,2048]{2,1,0:T(8,128)(2,1)} copy(bf16[1,704,2048]{2,1,0:T(8,128)(2,1)S(1)} %copy-done.1) | data formatting | bytes 5767168
  67.4 1.3 %copy-done = bf16[1,704,2048]{2,1,0:T(8,128)(2,1)S(1)} copy-done((bf16[1,704,2048]{2,1,0:T(8,128)(2,1)S(1)}, bf16[1,704,2048]{2,1,0:T(8,128)(2,1)}, u32[]{:S(2)}) %copy-start) | copy-done | bytes 2883608
  68.7 1.6 %copy.28 = bf16[1,704,2048]{2,1,0:T(8,128)(2,1)} copy(bf16[1,704,2048]{2,1,0:T(8,128)(2,1)S(1)} %copy-done) | data formatting | bytes 5767168
  (2 shorter events, 0.0 us)
Async XLA Ops:
  61.9 3.9 %copy-start.1 = (bf16[1,704,2048]{2,1,0:T(8,128)(2,1)S(1)}, bf16[1,704,2048]{2,1,0:T(8,128)(2,1)}, u32[]{:S(2)}) copy-start(bf16[1,704,2048]{2,1,0:T(8,128)(2,1)} %get-tuple-element.40) | copy-start | bytes 8650756
  65.8 2.9 %copy-start = (bf16[1,704,2048]{2,1,0:T(8,128)(2,1)S(1)}, bf16[1,704,2048]{2,1,0:T(8,128)(2,1)}, u32[]{:S(2)}) copy-start(bf16[1,704,2048]{2,1,0:T(8,128)(2,1)} %get-tuple-element.41) | copy-start | bytes 8650756

commit v2 on v1

v2 whole, which is shorter than its diff:
```python
import functools
import math

import jax
import jax.numpy as jnp
from jax import lax
from jax.experimental import pallas as pl
from jax.experimental.pallas import tpu as pltpu
from jax.sharding import PartitionSpec as P

EXP_DEV = 2
CORES = 2
MESH = pl.DeviceIdType.MESH
F32 = jnp.float32
BF16 = jnp.bfloat16


def dot(left, right, lhs_dim, rhs_dim):
    return lax.dot_general(
        left, right, (((lhs_dim,), (rhs_dim,)), ((), ())), preferred_element_type=F32
    )


def kernel(
    shape, tok, dmx, ids, wts, gate_hbm, up_hbm, down_hbm,
    mixed_out, route_out, dtok_out, xs_out, ds_out, hw_out, dg_out, du_out, *scratch,
):
    n_dp, side, n_z, rows, half, row_parts, tile, chunks = shape
    scratch = list(scratch)

    def take(count):
        taken = scratch[:count]
        del scratch[:count]
        return taken

    xs, ds, wg, wu, wd, gate, up, hidf, dhid, hw, dg, du, mine, weight_of = take(14)
    turned = take(3)
    count = len(chunks)
    ps, pr, acc, sb, ra, sc, rb, zb, zf, rz, ag = [take(count) for _ in range(11)]
    send_sem, recv_sem, load_sem, store_sem = take(4)
    dp = lax.axis_index("dp")
    column = lax.axis_index("expert")
    core = lax.rem(column, CORES)
    z = column // CORES
    step_a = 1 + core * (side - 1)
    step_b = side - core * (side - 1)
    a = lax.rem(dp // step_a, side)
    b = lax.rem(dp // step_b, side)

    def block_of(a_index, b_index):
        return a_index * step_a + b_index * step_b

    def turn(value, by, size):
        return lax.rem(value + by + size, size)

    sibling = (dp, column + 1 - 2 * core)

    def peer_a(by):
        return (block_of(turn(a, by, side), b), column)

    def peer_b(by):
        return (block_of(a, turn(b, by, side)), column)

    def peer_z(by):
        return (dp, turn(z, by, n_z) * CORES + core)

    partners = [sibling]
    partners += [peer_a(k) for k in range(1, side)]
    partners += [peer_b(k) for k in range(1, side)]
    partners += [peer_z(k) for k in range(1, n_z)]

    loads = []
    for number, (source, target) in enumerate(((gate_hbm, wg), (up_hbm, wu), (down_hbm, wd))):
        loads.append(pltpu.make_async_copy(source.at[0], target, load_sem.at[number]))
        loads[-1].start()

    used = [0]
    sent = []

    def send(source, target, device):
        copy = pltpu.make_async_remote_copy(
            src_ref=source, dst_ref=target, send_sem=send_sem.at[used[0]],
            recv_sem=recv_sem.at[used[0]], device_id=device, device_id_type=MESH,
        )
        used[0] += 1
        copy.start()
        sent.append(copy)
        return copy

    barrier = pltpu.get_barrier_semaphore()
    for partner in partners:
        pl.semaphore_signal(barrier, inc=1, device_id=partner, device_id_type=MESH)
    for part in range(CORES):
        xs[part, dp] = tok[:, part * half : (part + 1) * half]
        ds[part, dp] = dmx[:, part * half : (part + 1) * half]
    pl.semaphore_wait(barrier, len(partners))

    from_a, from_b, from_ab, from_core = [], [], [], []
    for buffer in (xs, ds):
        own = buffer.at[core, dp]
        from_a.append([send(own, own, peer_a(k)) for k in range(1, side)])
        from_b.append([send(own, own, peer_b(k)) for k in range(1, side)])
    for number, buffer in enumerate((xs, ds)):
        from_ab.append([])
        from_core.append([])
        for k in range(1, side):
            from_a[number][k - 1].wait_recv()
            got = buffer.at[core, block_of(turn(a, -k, side), b)]
            for m in range(1, side):
                from_ab[number].append(send(got, got, peer_b(m)))
            from_core[number].append(send(got, got, sibling))

    def finish_gather(number, buffer):
        for k in range(1, side):
            from_b[number][k - 1].wait_recv()
            got = buffer.at[core, block_of(a, turn(b, -k, side))]
            from_core[number].append(send(got, got, sibling))
        for k in range(1, side):
            for m in range(1, side):
                from_ab[number][(k - 1) * (side - 1) + m - 1].wait_recv()
                got = buffer.at[core, block_of(turn(a, -k, side), turn(b, -m, side))]
                from_core[number].append(send(got, got, sibling))

    def whole(buffer, part):
        return buffer[part].reshape(n_dp * rows, half)

    pieces = n_dp // EXP_DEV
    expert = column * EXP_DEV + dp // pieces
    piece = lax.rem(dp, pieces)
    choices = ids.shape[0]
    spread = (
        lax.rem(lax.broadcasted_iota(jnp.int32, (choices, 128), 1), 8)
        == lax.broadcasted_iota(jnp.int32, (choices, 128), 0)
    ).astype(F32)

    def spread_lanes(value):
        return lax.dot_general(
            value, spread, (((0,), (0,)), ((), ())),
            precision=lax.Precision.HIGHEST, preferred_element_type=F32,
        )

    lanes = lax.broadcasted_iota(jnp.int32, (n_dp * rows, 128), 1)
    hit = ids[...] == expert
    named = spread_lanes(hit.astype(F32))
    weight_of[...] = jnp.broadcast_to(
        jnp.sum(
            jnp.where(lanes < 8, spread_lanes(jnp.where(hit, wts[...], 0.0)), 0.0),
            axis=1, keepdims=True,
        ),
        (n_dp * rows, 128),
    )
    mine[...] = jnp.where(lax.rem(lanes // 8, 8) == piece, named, 0.0)

    stores = []

    def keep(source, target):
        stores.append(pltpu.make_async_copy(source, target, store_sem.at[len(stores)]))
        stores[-1].start()

    finish_gather(0, xs)
    for copy in from_core[0]:
        copy.wait_recv()
    loads[0].wait()
    gate[...] = dot(whole(xs, 0), wg[:, :half], 1, 1) + dot(whole(xs, 1), wg[:, half:], 1, 1)
    finish_gather(1, ds)
    loads[1].wait()
    up[...] = dot(whole(xs, 0), wu[:, :half], 1, 1) + dot(whole(xs, 1), wu[:, half:], 1, 1)
    strip = rows // 2

    @pl.loop(0, 2 * n_dp)
    def forward(index):
        span = pl.ds(pl.multiple_of(index * strip, strip), strip)
        gate_value = gate[span, :]
        up_value = up[span, :]
        sigmoid_gate = 1.0 / (1.0 + jnp.exp(-gate_value))
        activated = gate_value * sigmoid_gate
        hidden = activated * up_value
        hw[span, :] = (weight_of[span, :1] * hidden).astype(BF16)
        hidf[span, :] = hidden
        up[span, :] = activated
        gate[span, :] = up_value * sigmoid_gate * (1.0 + gate_value * (1.0 - sigmoid_gate))

    def product(q, columns):
        if q == 0:
            return dot(hw[...], wd[:, columns], 1, 0)
        return dot(dg[...], wg[:, columns], 1, 0) + dot(du[...], wu[:, columns], 1, 0)

    def other_half(q):
        first, wide = chunks[q]

        @pl.loop(0, wide // tile)
        def columns(t):
            start = pl.multiple_of((1 - core) * half + first + t * tile, tile)
            value = product(q, pl.ds(start, tile)).astype(BF16)
            ps[q][:, :, pl.ds(pl.multiple_of(t * tile, tile), tile)] = value.reshape(
                n_dp, rows, tile
            )

        return send(ps[q], pr[q], sibling)

    def own_half(q):
        first, wide = chunks[q]

        @pl.loop(0, wide // tile)
        def columns(t):
            start = pl.multiple_of(core * half + first + t * tile, tile)
            value = product(q, pl.ds(start, tile))
            acc[q][:, :, pl.ds(pl.multiple_of(t * tile, tile), tile)] = value.reshape(
                n_dp, rows, tile
            )

    def pair_done(q, copy):
        copy.wait_recv()
        wide = chunks[q][1]

        @pl.loop(0, n_dp)
        def add(block):
            total = acc[q][block, :, :wide] + pr[q][block].astype(F32)
            acc[q][block, :, :wide] = total
            sb[q][block, :, :wide] = total.astype(BF16)
            if acc[q].shape[2] > wide:
                sb[q][block, :, wide:] = acc[q][block, :, wide:].astype(BF16)

        copies = []
        for k in range(1, side):
            for m in range(side):
                source = sb[q].at[block_of(turn(a, k, side), m)]
                copies.append(send(source, ra[q].at[k - 1, m], peer_a(k)))
        return copies

    def first_done(q, copies):
        for copy in copies:
            copy.wait_recv()
        following = []
        for m in range(1, side + 1):
            goal = turn(b, m, side)
            total = acc[q][block_of(a, goal)]
            for k in range(1, side):
                total = total + ra[q][k - 1, goal].astype(F32)
            if m < side:
                sc[q][m - 1] = total.astype(BF16)
                following.append(send(sc[q].at[m - 1], rb[q].at[m - 1], peer_b(m)))
            else:
                acc[q][block_of(a, b)] = total
        return following

    def second_done(q, copies):
        for copy in copies:
            copy.wait_recv()
        total = acc[q][block_of(a, b)]
        for k in range(1, side):
            total = total + rb[q][k - 1].astype(F32)
        high, wide = zb[q].shape[1:]
        for part in range(n_z):
            top = (part % row_parts) * high
            left = (part // row_parts) * wide
            value = total[top : top + high, left : left + wide]
            zf[q][part] = value
            zb[q][part] = value.astype(BF16)
        return [
            send(zb[q].at[turn(z, k, n_z)], rz[q].at[k - 1], peer_z(k)) for k in range(1, n_z)
        ]

    def third_done(q, copies):
        for copy in copies:
            copy.wait_recv()
        total = zf[q][z]
        for k in range(1, n_z):
            total = total + rz[q][k - 1].astype(F32)
        ag[q][core, z] = total.astype(BF16)
        own = ag[q].at[core, z]
        following = [send(own, own, peer_z(k)) for k in range(1, n_z)]
        return following, [send(own, own, sibling)]

    def fourth_done(q, copies, shared):
        for k in range(1, n_z):
            copies[k - 1].wait_recv()
            got = ag[q].at[core, turn(z, -k, n_z)]
            shared.append(send(got, got, sibling))

    loads[2].wait()
    pair0 = other_half(0)
    own_half(0)
    step0 = pair_done(0, pair0)
    for copy in from_core[1]:
        copy.wait_recv()
    dhid[...] = dot(whole(ds, 0), wd[:, :half], 1, 1) + dot(whole(ds, 1), wd[:, half:], 1, 1)

    @pl.loop(0, 2 * n_dp)
    def backward(index):
        span = pl.ds(pl.multiple_of(index * strip, strip), strip)
        lane = lax.broadcasted_iota(jnp.int32, (strip, 128), 1)
        plain = dhid[span, :]
        paired = jnp.sum(hidf[span, :] * plain, axis=1, keepdims=True)
        d_hidden = weight_of[span, :1] * plain
        dg[span, :] = (d_hidden * gate[span, :]).astype(BF16)
        du[span, :] = (d_hidden * up[span, :]).astype(BF16)
        leading = paired.astype(BF16).astype(F32)
        share = jnp.where(lane < 64, leading, paired - leading) * mine[span, :]
        block = index // 2
        inner = pl.ds(pl.multiple_of(lax.rem(index, 2) * strip, strip), strip)
        wide = chunks[1][1]
        acc[1][block, inner, wide : wide + 128] = share
        if acc[1].shape[2] > wide + 128:
            acc[1][block, inner, wide + 128 :] = jnp.zeros(
                (strip, acc[1].shape[2] - wide - 128), F32
            )

    pair1 = other_half(1)
    step0 = first_done(0, step0)
    own_half(1)
    step1 = pair_done(1, pair1)
    pair2 = other_half(2)
    step0 = second_done(0, step0)
    own_half(2)
    step2 = pair_done(2, pair2)
    step1 = first_done(1, step1)
    keep(xs, xs_out)
    keep(ds, ds_out)
    for number, (source, target) in enumerate(((hw, hw_out), (dg, dg_out), (du, du_out))):
        turned[number][...] = jnp.transpose(source[...])
        keep(turned[number], target)
    step0, shared0 = third_done(0, step0)
    step2 = first_done(2, step2)
    step1 = second_done(1, step1)
    step2 = second_done(2, step2)
    fourth_done(0, step0, shared0)
    step1, shared1 = third_done(1, step1)
    step2, shared2 = third_done(2, step2)
    fourth_done(1, step1, shared1)
    fourth_done(2, step2, shared2)

    for q, (target, shared) in enumerate(
        ((mixed_out, shared0), (dtok_out, shared1), (dtok_out, shared2))
    ):
        for copy in shared:
            copy.wait_recv()
        first, width = chunks[q]
        high = zb[q].shape[1]
        for part in range(row_parts):
            span = slice(part * high, (part + 1) * high)
            routes = 0.0
            for side_core in range(CORES):
                strips = [ag[q][side_core, k * row_parts + part] for k in range(n_z // row_parts)]
                line = strips[0] if len(strips) == 1 else jnp.concatenate(strips, axis=1)
                left = side_core * half + first
                target[span, left : left + width] = line[:, :width]
                if q == 1:
                    routes = routes + line[:, width : width + 128].astype(F32)
            if q == 1:
                for by in (64, 32, 16, 8):
                    routes = routes + pltpu.roll(routes, by, 1)
                route_out[span, :] = routes
    for copy in sent:
        copy.wait_send()
    for copy in stores:
        copy.wait()


def finish(mixed, route, d_tokens, xs, ds, hw, dg, du, mixed_out, route_out, dtok_out, gg, gu, gd):
    @pl.when(pl.program_id(0) == 0)
    def once():
        mixed_out[...] = mixed[...]
        dtok_out[...] = d_tokens[...]
        route_out[...] = jnp.transpose(route[...])[: route_out.shape[0]]

    total_rows = hw.shape[1]
    x_tile = xs[0].reshape(total_rows, xs.shape[3])
    d_tile = ds[0].reshape(total_rows, ds.shape[3])
    gd[0] = dot(hw[...], d_tile, 1, 0).astype(BF16)
    gg[0] = dot(dg[...], x_tile, 1, 0).astype(BF16)
    gu[0] = dot(du[...], x_tile, 1, 0).astype(BF16)


def body(tokens, d_mixed, route_ids, route_weight, gate_weight, up_weight, down_weight):
    n_dp = lax.axis_size("dp")
    n_z = lax.axis_size("expert") // CORES
    side = math.isqrt(n_dp)
    rows, width = tokens.shape
    choices = route_ids.shape[1]
    hid = gate_weight.shape[1]
    half = width // CORES
    tile = 256
    row_parts = min(n_z, rows // 16)
    col_parts = n_z // row_parts
    high = rows // row_parts
    chunks = ((0, half), (0, half // 2), (half // 2, half // 2))
    plain_widths = tuple(wide for _, wide in chunks)
    widths = (half, half // 2 + 128 * col_parts, half // 2)
    total_rows = n_dp * rows

    def vmem(*dims, dtype=BF16):
        return pltpu.VMEM(dims, dtype)

    def each(make, sizes=widths):
        return [make(w) for w in sizes]

    scratch = [vmem(CORES, n_dp, rows, half)] * 2
    scratch += [vmem(hid, width)] * 3
    scratch += [vmem(total_rows, hid, dtype=F32)] * 4
    scratch += [vmem(total_rows, hid)] * 3
    scratch += [vmem(total_rows, 128, dtype=F32)] * 2
    scratch += [vmem(hid, total_rows)] * 3
    scratch += each(lambda w: vmem(n_dp, rows, w), plain_widths) * 2
    scratch += each(lambda w: vmem(n_dp, rows, w, dtype=F32))
    scratch += each(lambda w: vmem(n_dp, rows, w))
    scratch += each(lambda w: vmem(side - 1, side, rows, w))
    scratch += each(lambda w: vmem(side - 1, rows, w))
    scratch += each(lambda w: vmem(side - 1, rows, w))
    scratch += each(lambda w: vmem(n_z, high, w // col_parts))
    scratch += each(lambda w: vmem(n_z, high, w // col_parts, dtype=F32))
    scratch += each(lambda w: vmem(n_z - 1, high, w // col_parts))
    scratch += each(lambda w: vmem(CORES, n_z, high, w // col_parts))
    gather = 2 * (2 * (side - 1) + (side - 1) ** 2 + n_dp - 1)
    reduce = len(chunks) * (1 + (side - 1) * side + side - 1 + 2 * (n_z - 1) + n_z)
    copies = gather + reduce
    scratch += [pltpu.SemaphoreType.DMA((copies,))] * 2
    scratch += [pltpu.SemaphoreType.DMA((3,)), pltpu.SemaphoreType.DMA((5,))]

    in_vmem = pl.BlockSpec(memory_space=pltpu.VMEM)
    anywhere = pl.BlockSpec(memory_space=pl.ANY)
    flat = jax.ShapeDtypeStruct((rows, width), BF16)
    gathered = jax.ShapeDtypeStruct((CORES, n_dp, rows, half), BF16)
    left = jax.ShapeDtypeStruct((hid, total_rows), BF16)
    shape = (n_dp, side, n_z, rows, half, row_parts, tile, chunks)
    results = pl.pallas_call(
        functools.partial(kernel, shape),
        out_shape=(flat, jax.ShapeDtypeStruct((rows, 128), F32), flat)
        + (gathered,) * 2 + (left,) * 3,
        in_specs=[in_vmem] * 4 + [anywhere] * 3,
        out_specs=(in_vmem,) * 3 + (anywhere,) * 5,
        scratch_shapes=scratch,
        compiler_params=pltpu.CompilerParams(
            collective_id=0, has_side_effects=True, vmem_limit_bytes=60 * 1024 * 1024
        ),
        cost_estimate=pl.CostEstimate(
            flops=12 * total_rows * hid * width,
            bytes_accessed=6 * hid * width,
            transcendentals=total_rows * hid,
        ),
    )(tokens, d_mixed, route_ids.T, route_weight.T, gate_weight, up_weight, down_weight)

    per_half = half // tile

    def fixed(*dims):
        return pl.BlockSpec(dims, lambda j: (0,) * len(dims))

    rows_tile = pl.BlockSpec(
        (1, n_dp, rows, tile), lambda j: (j // per_half, 0, 0, lax.rem(j, per_half))
    )
    grad_tile = pl.BlockSpec((1, hid, tile), lambda j: (0, 0, j))
    grad = jax.ShapeDtypeStruct((1, hid, width), BF16)
    mixed, route, d_tokens, grad_gate, grad_up, grad_down = pl.pallas_call(
        finish,
        grid=(width // tile,),
        out_shape=(flat, jax.ShapeDtypeStruct((choices, rows), F32), flat, grad, grad, grad),
        in_specs=[fixed(rows, width), fixed(rows, 128), fixed(rows, width)]
        + [rows_tile] * 2 + [fixed(hid, total_rows)] * 3,
        out_specs=(fixed(rows, width), fixed(choices, rows), fixed(rows, width))
        + (grad_tile,) * 3,
        compiler_params=pltpu.CompilerParams(vmem_limit_bytes=60 * 1024 * 1024),
        cost_estimate=pl.CostEstimate(
            flops=6 * total_rows * hid * width,
            bytes_accessed=6 * hid * width,
            transcendentals=0,
        ),
    )(*results)
    return mixed, route.T, d_tokens, grad_gate, grad_up, grad_down


def solution(mesh):
    row, whole, block = P("dp", None), P(), P(("expert", "dp"), None, None)
    return jax.shard_map(
        body,
        mesh=mesh,
        in_specs=(row, row, whole, whole, block, block, block),
        out_specs=(row, row, row, block, block, block),
        check_vma=False,
    )
```

time: 70.6 us -> 63.2 us (0.90)
  local copies, waits for them, and re-layouts: 16 us -> 0 us
  Pallas kernels: 53.5 us -> 62.3 us
    unnamed x10 -> x0, local copies, waits for them, and re-layouts: 13.1 us -> none
    pallas_call x0 -> x1, Pallas kernels: none -> 9.14 us  [body(): pl.pallas_call(finish, grid=(width // tile,), out_shape=(flat, jax.ShapeD...]
    another operation x4 -> x0, local copies, waits for them, and re-layouts: 1.53 us -> none  [the longest x2 0.77 us: body(): wts = jnp.tile(jnp.pad(route_weight, pad), (1, 16))]
    pad x2 -> x0, local copies, waits for them, and re-layouts: 1.4 us -> none  [the longest x1 0.7 us: body(): ids = jnp.tile(jnp.pad(route_ids, pad, constant_values=-1), (1, 16))]
where the time goes in v2:
time: 63.2 us; the launch traced here: 62.9 us
  Pallas kernels  62.3 us (99%)
  between operations  0.64 us (1%)
    pallas_call x1, Pallas kernels, body(): pl.pallas_call(functools.partial(kernel, shape), out_shape=(flat, jax.Sha...  53.2 us
    pallas_call x1, Pallas kernels, body(): pl.pallas_call(finish, grid=(width // tile,), out_shape=(flat, jax.ShapeD...  9.14 us

profile of v2, /device:TPU:0, one launch (start us, length us, event | category | flops | bytes accessed | tf_op | source)
XLA Modules:
  0.0 62.9 jit_solution(793367011984191390)
XLA Ops:
  0.6 53.2 %shard_map.118 = (bf16[64,2048]{1,0:T(8,128)(2,1)}, f32[64,128]{1,0:T(8,128)}, bf16[64,2048]{1,0:T(8,128)(2,1)}, bf16[2,4,64,1024]{3,2,1,0:T(8,128)(2,1)}, bf16[...) custom-call(bf16[64,2048]{1,0:T(8,128)(2,1)} %tok.1, ...), custom_call_target="tpu_custom_call" | custom-call | flops 4429185024 | bytes 8650752 | tf_op jit(solution)/shard_map/pallas_call | solution.py:426
  53.8 9.1 %shard_map.119 = (bf16[64,2048]{1,0:T(8,128)(2,1)}, f32[6,64]{1,0:T(8,128)}, bf16[64,2048]{1,0:T(8,128)(2,1)}, bf16[1,704,2048]{2,1,0:T(8,128)(2,1)}, bf16[1,704...) custom-call(bf16[64,2048]{1,0:T(8,128)(2,1)} %get-tuple-element.20.mixed, f32[64,128]{1,0:T(8,128)} %get-tuple-element.21.route, ...), custom_call_target="tpu_custom_call" | custom-call | flops 2214592512 | bytes 8650752 | tf_op jit(solution)/shard_map/pallas_call | solution.py:453

commit v3 on v2

--- a/solution.py
+++ b/solution.py
@@ -33,8 +33,9 @@
         del scratch[:count]
         return taken
 
-    xs, ds, wg, wu, wd, gate, up, hidf, dhid, hw, dg, du, mine, weight_of = take(14)
+    xs, ds, wg, wu, wd, gate, up, hidf, dhid, ids8, wts8, paired = take(12)
     turned = take(3)
+    hw, dg, du = take(3)
     count = len(chunks)
     ps, pr, acc, sb, ra, sc, rb, zb, zf, rz, ag = [take(count) for _ in range(11)]
     send_sem, recv_sem, load_sem, store_sem = take(4)
@@ -96,11 +97,8 @@
     pl.semaphore_wait(barrier, len(partners))
 
     from_a, from_b, from_ab, from_core = [], [], [], []
-    for buffer in (xs, ds):
-        own = buffer.at[core, dp]
-        from_a.append([send(own, own, peer_a(k)) for k in range(1, side)])
-        from_b.append([send(own, own, peer_b(k)) for k in range(1, side)])
-    for number, buffer in enumerate((xs, ds)):
+
+    def pass_on(number, buffer):
         from_ab.append([])
         from_core.append([])
         for k in range(1, side):
@@ -109,6 +107,13 @@
             for m in range(1, side):
                 from_ab[number].append(send(got, got, peer_b(m)))
             from_core[number].append(send(got, got, sibling))
+
+    for buffer in (xs, ds):
+        own = buffer.at[core, dp]
+        from_a.append([send(own, own, peer_a(k)) for k in range(1, side)])
+        from_b.append([send(own, own, peer_b(k)) for k in range(1, side)])
+        if buffer is xs:
+            pass_on(0, xs)
 
     def finish_gather(number, buffer):
         for k in range(1, side):
@@ -128,28 +133,12 @@
     expert = column * EXP_DEV + dp // pieces
     piece = lax.rem(dp, pieces)
     choices = ids.shape[0]
-    spread = (
-        lax.rem(lax.broadcasted_iota(jnp.int32, (choices, 128), 1), 8)
-        == lax.broadcasted_iota(jnp.int32, (choices, 128), 0)
-    ).astype(F32)
-
-    def spread_lanes(value):
-        return lax.dot_general(
-            value, spread, (((0,), (0,)), ((), ())),
-            precision=lax.Precision.HIGHEST, preferred_element_type=F32,
-        )
-
-    lanes = lax.broadcasted_iota(jnp.int32, (n_dp * rows, 128), 1)
-    hit = ids[...] == expert
-    named = spread_lanes(hit.astype(F32))
-    weight_of[...] = jnp.broadcast_to(
-        jnp.sum(
-            jnp.where(lanes < 8, spread_lanes(jnp.where(hit, wts[...], 0.0)), 0.0),
-            axis=1, keepdims=True,
-        ),
-        (n_dp * rows, 128),
-    )
-    mine[...] = jnp.where(lax.rem(lanes // 8, 8) == piece, named, 0.0)
+    ids8[...] = jnp.full(ids8.shape, -1, jnp.int32)
+    ids8[:choices, :] = ids[...]
+    wts8[...] = jnp.zeros(wts8.shape, F32)
+    wts8[:choices, :] = wts[...]
+    named = ids8[...] == expert
+    weight = jnp.sum(jnp.where(named, wts8[...], 0.0), axis=0, keepdims=True)
 
     stores = []
 
@@ -161,13 +150,14 @@
     for copy in from_core[0]:
         copy.wait_recv()
     loads[0].wait()
-    gate[...] = dot(whole(xs, 0), wg[:, :half], 1, 1) + dot(whole(xs, 1), wg[:, half:], 1, 1)
-    finish_gather(1, ds)
+    gate[...] = dot(wg[:, :half], whole(xs, 0), 1, 1) + dot(wg[:, half:], whole(xs, 1), 1, 1)
+    pass_on(1, ds)
     loads[1].wait()
-    up[...] = dot(whole(xs, 0), wu[:, :half], 1, 1) + dot(whole(xs, 1), wu[:, half:], 1, 1)
-    strip = rows // 2
-
-    @pl.loop(0, 2 * n_dp)
+    up[...] = dot(wu[:, :half], whole(xs, 0), 1, 1) + dot(wu[:, half:], whole(xs, 1), 1, 1)
+    hid = gate.shape[0]
+    strip = 16 * max(k for k in range(1, 12) if hid // 16 % k == 0)
+
+    @pl.loop(0, hid // strip)
     def forward(index):
         span = pl.ds(pl.multiple_of(index * strip, strip), strip)
         gate_value = gate[span, :]
@@ -175,10 +165,12 @@
         sigmoid_gate = 1.0 / (1.0 + jnp.exp(-gate_value))
         activated = gate_value * sigmoid_gate
         hidden = activated * up_value
-        hw[span, :] = (weight_of[span, :1] * hidden).astype(BF16)
+        turned[0][span, :] = (weight * hidden).astype(BF16)
         hidf[span, :] = hidden
         up[span, :] = activated
         gate[span, :] = up_value * sigmoid_gate * (1.0 + gate_value * (1.0 - sigmoid_gate))
+
+    hw[...] = jnp.transpose(turned[0][...])
 
     def product(q, columns):
         if q == 0:
@@ -280,31 +272,37 @@
 
     loads[2].wait()
     pair0 = other_half(0)
+    finish_gather(1, ds)
     own_half(0)
     step0 = pair_done(0, pair0)
     for copy in from_core[1]:
         copy.wait_recv()
-    dhid[...] = dot(whole(ds, 0), wd[:, :half], 1, 1) + dot(whole(ds, 1), wd[:, half:], 1, 1)
-
-    @pl.loop(0, 2 * n_dp)
+    dhid[...] = dot(wd[:, :half], whole(ds, 0), 1, 1) + dot(wd[:, half:], whole(ds, 1), 1, 1)
+    paired[...] = jnp.zeros(paired.shape, F32)
+
+    @pl.loop(0, hid // strip)
     def backward(index):
         span = pl.ds(pl.multiple_of(index * strip, strip), strip)
-        lane = lax.broadcasted_iota(jnp.int32, (strip, 128), 1)
         plain = dhid[span, :]
-        paired = jnp.sum(hidf[span, :] * plain, axis=1, keepdims=True)
-        d_hidden = weight_of[span, :1] * plain
-        dg[span, :] = (d_hidden * gate[span, :]).astype(BF16)
-        du[span, :] = (d_hidden * up[span, :]).astype(BF16)
-        leading = paired.astype(BF16).astype(F32)
-        share = jnp.where(lane < 64, leading, paired - leading) * mine[span, :]
-        block = index // 2
-        inner = pl.ds(pl.multiple_of(lax.rem(index, 2) * strip, strip), strip)
-        wide = chunks[1][1]
-        acc[1][block, inner, wide : wide + 128] = share
-        if acc[1].shape[2] > wide + 128:
-            acc[1][block, inner, wide + 128 :] = jnp.zeros(
-                (strip, acc[1].shape[2] - wide - 128), F32
-            )
+        paired[...] += jnp.sum(hidf[span, :] * plain, axis=0, keepdims=True)
+        d_hidden = weight * plain
+        turned[1][span, :] = (d_hidden * gate[span, :]).astype(BF16)
+        turned[2][span, :] = (d_hidden * up[span, :]).astype(BF16)
+
+    dg[...] = jnp.transpose(turned[1][...])
+    du[...] = jnp.transpose(turned[2][...])
+    share = paired[...]
+    leading = share.astype(BF16).astype(F32)
+    kept = jnp.where(named, leading, 0.0)
+    rest = jnp.where(named, share - leading, 0.0)
+    groups = [jnp.where(piece == k, kept, 0.0) for k in range(8)]
+    groups += [jnp.where(piece == k, rest, 0.0) for k in range(8)]
+    lanes = jnp.transpose(jnp.concatenate(groups, axis=0)).reshape(n_dp, rows, 128)
+    wide = chunks[1][1]
+    acc[1][:, :, wide : wide + 128] = lanes
+    extra = acc[1].shape[2] - wide - 128
+    if extra:
+        acc[1][:, :, wide + 128 :] = jnp.zeros((n_dp, rows, extra), F32)
 
     pair1 = other_half(1)
     step0 = first_done(0, step0)
@@ -317,9 +315,8 @@
     step1 = first_done(1, step1)
     keep(xs, xs_out)
     keep(ds, ds_out)
-    for number, (source, target) in enumerate(((hw, hw_out), (dg, dg_out), (du, du_out))):
-        turned[number][...] = jnp.transpose(source[...])
-        keep(turned[number], target)
+    for source, target in zip(turned, (hw_out, dg_out, du_out)):
+        keep(source, target)
     step0, shared0 = third_done(0, step0)
     step2 = first_done(2, step2)
     step1 = second_done(1, step1)
@@ -357,19 +354,45 @@
         copy.wait()
 
 
-def finish(mixed, route, d_tokens, xs, ds, hw, dg, du, mixed_out, route_out, dtok_out, gg, gu, gd):
-    @pl.when(pl.program_id(0) == 0)
-    def once():
-        mixed_out[...] = mixed[...]
-        dtok_out[...] = d_tokens[...]
-        route_out[...] = jnp.transpose(route[...])[: route_out.shape[0]]
-
+def finish(
+    tile, route, mixed, d_tokens, xs, ds, hw, dg, du, route_out, mixed_out, dtok_out, gg, gu, gd,
+    x_in, d_in, hw_in, dg_in, du_in, stage, load_sem, store_sem,
+):
+    def copy(source, target, sem):
+        made = pltpu.make_async_copy(source, target, sem)
+        made.start()
+        return made
+
+    moves = ((hw, hw_in), (ds, d_in), (dg, dg_in), (xs, x_in), (du, du_in))
+    loads = [copy(source, target, load_sem.at[k]) for k, (source, target) in enumerate(moves)]
+    stores = [copy(mixed, mixed_out, store_sem.at[0]), copy(d_tokens, dtok_out, store_sem.at[1])]
+    route_out[...] = jnp.transpose(route[...])[: route_out.shape[0]]
+    half = xs.shape[3]
     total_rows = hw.shape[1]
-    x_tile = xs[0].reshape(total_rows, xs.shape[3])
-    d_tile = ds[0].reshape(total_rows, ds.shape[3])
-    gd[0] = dot(hw[...], d_tile, 1, 0).astype(BF16)
-    gg[0] = dot(dg[...], x_tile, 1, 0).astype(BF16)
-    gu[0] = dot(du[...], x_tile, 1, 0).astype(BF16)
+    for number, (left, buffer, target, ready) in enumerate(
+        ((hw_in, d_in, gd, 2), (dg_in, x_in, gg, 2), (du_in, x_in, gu, 1))
+    ):
+        for _ in range(ready):
+            loads.pop(0).wait()
+        for part in range(CORES):
+
+            @pl.loop(0, half // tile)
+            def columns(t):
+                right = buffer[part, :, :, pl.ds(pl.multiple_of(t * tile, tile), tile)]
+                start = pl.multiple_of(part * half + t * tile, tile)
+                stage[number, :, pl.ds(start, tile)] = dot(
+                    left[...], right.reshape(total_rows, tile), 1, 0
+                ).astype(BF16)
+
+            span = pl.ds(part * half, half)
+            stores.append(
+                copy(
+                    stage.at[number, :, span], target.at[0, :, span],
+                    store_sem.at[2 + CORES * number + part],
+                )
+            )
+    for store in stores:
+        store.wait()
 
 
 def body(tokens, d_mixed, route_ids, route_weight, gate_weight, up_weight, down_weight):
@@ -397,10 +420,11 @@
 
     scratch = [vmem(CORES, n_dp, rows, half)] * 2
     scratch += [vmem(hid, width)] * 3
-    scratch += [vmem(total_rows, hid, dtype=F32)] * 4
+    scratch += [vmem(hid, total_rows, dtype=F32)] * 4
+    scratch += [vmem(8, total_rows, dtype=jnp.int32), vmem(8, total_rows, dtype=F32)]
+    scratch += [vmem(1, total_rows, dtype=F32)]
+    scratch += [vmem(hid, total_rows)] * 3
     scratch += [vmem(total_rows, hid)] * 3
-    scratch += [vmem(total_rows, 128, dtype=F32)] * 2
-    scratch += [vmem(hid, total_rows)] * 3
     scratch += each(lambda w: vmem(n_dp, rows, w), plain_widths) * 2
     scratch += each(lambda w: vmem(n_dp, rows, w, dtype=F32))
     scratch += each(lambda w: vmem(n_dp, rows, w))
@@ -440,31 +464,23 @@
         ),
     )(tokens, d_mixed, route_ids.T, route_weight.T, gate_weight, up_weight, down_weight)
 
-    per_half = half // tile
-
-    def fixed(*dims):
-        return pl.BlockSpec(dims, lambda j: (0,) * len(dims))
-
-    rows_tile = pl.BlockSpec(
-        (1, n_dp, rows, tile), lambda j: (j // per_half, 0, 0, lax.rem(j, per_half))
-    )
-    grad_tile = pl.BlockSpec((1, hid, tile), lambda j: (0, 0, j))
+    mixed, route, d_tokens, *operands = results
     grad = jax.ShapeDtypeStruct((1, hid, width), BF16)
-    mixed, route, d_tokens, grad_gate, grad_up, grad_down = pl.pallas_call(
-        finish,
-        grid=(width // tile,),
-        out_shape=(flat, jax.ShapeDtypeStruct((choices, rows), F32), flat, grad, grad, grad),
-        in_specs=[fixed(rows, width), fixed(rows, 128), fixed(rows, width)]
-        + [rows_tile] * 2 + [fixed(hid, total_rows)] * 3,
-        out_specs=(fixed(rows, width), fixed(choices, rows), fixed(rows, width))
-        + (grad_tile,) * 3,
+    route, mixed, d_tokens, grad_gate, grad_up, grad_down = pl.pallas_call(
+        functools.partial(finish, 2 * tile),
+        out_shape=(jax.ShapeDtypeStruct((choices, rows), F32), flat, flat, grad, grad, grad),
+        in_specs=[in_vmem] + [anywhere] * 7,
+        out_specs=(in_vmem,) + (anywhere,) * 5,
+        scratch_shapes=[vmem(CORES, n_dp, rows, half)] * 2
+        + [vmem(hid, total_rows)] * 3
+        + [vmem(3, hid, width), pltpu.SemaphoreType.DMA((5,)), pltpu.SemaphoreType.DMA((8,))],
         compiler_params=pltpu.CompilerParams(vmem_limit_bytes=60 * 1024 * 1024),
         cost_estimate=pl.CostEstimate(
             flops=6 * total_rows * hid * width,
             bytes_accessed=6 * hid * width,
             transcendentals=0,
         ),
-    )(*results)
+    )(route, mixed, d_tokens, *operands)
     return mixed, route.T, d_tokens, grad_gate, grad_up, grad_down
 
 

time: 63.2 us -> 71.7 us (1.13)
  Pallas kernels: 62.3 us -> 70.9 us
    pallas_call x1, Pallas kernels: 9.14 us -> 18.5 us  [body(): pl.pallas_call(functools.partial(finish, 2 * tile), out_shape=(jax.ShapeD...]
    pallas_call x1, Pallas kernels: 53.2 us -> 52.4 us  [body(): pl.pallas_call(functools.partial(kernel, shape), out_shape=(flat, jax.Sha...]
where the time goes in v3:
time: 71.7 us; the launch traced here: 71.5 us
  Pallas kernels  70.9 us (99%)
    pallas_call x1, Pallas kernels, body(): pl.pallas_call(functools.partial(kernel, shape), out_shape=(flat, jax.Sha...  52.4 us
    pallas_call x1, Pallas kernels, body(): pl.pallas_call(functools.partial(finish, 2 * tile), out_shape=(jax.ShapeD...  18.5 us

profile of v3, /device:TPU:0, one launch (start us, length us, event | category | flops | bytes accessed | tf_op | source)
XLA Modules:
  0.0 71.5 jit_solution(10477651356581111908)
XLA Ops:
  0.6 52.4 %shard_map.118 = (bf16[64,2048]{1,0:T(8,128)(2,1)}, f32[64,128]{1,0:T(8,128)}, bf16[64,2048]{1,0:T(8,128)(2,1)}, bf16[2,4,64,1024]{3,2,1,0:T(8,128)(2,1)}, bf16[...) custom-call(bf16[64,2048]{1,0:T(8,128)(2,1)} %tok.1, ...), custom_call_target="tpu_custom_call" | custom-call | flops 4429185024 | bytes 8650752 | tf_op jit(solution)/shard_map/pallas_call | solution.py:450
  53.0 18.5 %shard_map.119 = (f32[6,64]{1,0:T(8,128)}, bf16[64,2048]{1,0:T(8,128)(2,1)}, bf16[64,2048]{1,0:T(8,128)(2,1)}, bf16[1,704,2048]{2,1,0:T(8,128)(2,1)}, bf16[1,704...) custom-call(f32[64,128]{1,0:T(8,128)} %get-tuple-element.20.route, bf16[64,2048]{1,0:T(8,128)(2,1)} %get-tuple-element.21.mixed, ...), custom_call_target="tpu_custom_call" | custom-call | flops 2214592512 | bytes 8650752 | tf_op jit(solution)/shard_map/pallas_call | solution.py:469

commit v4 on v3

--- a/solution.py
+++ b/solution.py
@@ -1,5 +1,4 @@
 import functools
-import math
 
 import jax
 import jax.numpy as jnp
@@ -25,7 +24,7 @@
     shape, tok, dmx, ids, wts, gate_hbm, up_hbm, down_hbm,
     mixed_out, route_out, dtok_out, xs_out, ds_out, hw_out, dg_out, du_out, *scratch,
 ):
-    n_dp, side, n_z, rows, half, row_parts, tile, chunks = shape
+    n_dp, n_z, rows, half, row_parts, tile, chunks = shape
     scratch = list(scratch)
 
     def take(count):
@@ -37,37 +36,25 @@
     turned = take(3)
     hw, dg, du = take(3)
     count = len(chunks)
-    ps, pr, acc, sb, ra, sc, rb, zb, zf, rz, ag = [take(count) for _ in range(11)]
+    ps, pr, acc, sb, rb, zb, zf, rz, ag = [take(count) for _ in range(9)]
     send_sem, recv_sem, load_sem, store_sem = take(4)
     dp = lax.axis_index("dp")
     column = lax.axis_index("expert")
     core = lax.rem(column, CORES)
     z = column // CORES
-    step_a = 1 + core * (side - 1)
-    step_b = side - core * (side - 1)
-    a = lax.rem(dp // step_a, side)
-    b = lax.rem(dp // step_b, side)
-
-    def block_of(a_index, b_index):
-        return a_index * step_a + b_index * step_b
-
     def turn(value, by, size):
         return lax.rem(value + by + size, size)
 
     sibling = (dp, column + 1 - 2 * core)
 
-    def peer_a(by):
-        return (block_of(turn(a, by, side), b), column)
-
-    def peer_b(by):
-        return (block_of(a, turn(b, by, side)), column)
+    def peer_dp(by):
+        return (turn(dp, by, n_dp), column)
 
     def peer_z(by):
         return (dp, turn(z, by, n_z) * CORES + core)
 
     partners = [sibling]
-    partners += [peer_a(k) for k in range(1, side)]
-    partners += [peer_b(k) for k in range(1, side)]
+    partners += [peer_dp(k) for k in range(1, n_dp)]
     partners += [peer_z(k) for k in range(1, n_z)]
 
     loads = []
@@ -96,35 +83,16 @@
         ds[part, dp] = dmx[:, part * half : (part + 1) * half]
     pl.semaphore_wait(barrier, len(partners))
 
-    from_a, from_b, from_ab, from_core = [], [], [], []
-
-    def pass_on(number, buffer):
-        from_ab.append([])
-        from_core.append([])
-        for k in range(1, side):
-            from_a[number][k - 1].wait_recv()
-            got = buffer.at[core, block_of(turn(a, -k, side), b)]
-            for m in range(1, side):
-                from_ab[number].append(send(got, got, peer_b(m)))
-            from_core[number].append(send(got, got, sibling))
-
+    from_dp, from_core = [], [[], []]
     for buffer in (xs, ds):
         own = buffer.at[core, dp]
-        from_a.append([send(own, own, peer_a(k)) for k in range(1, side)])
-        from_b.append([send(own, own, peer_b(k)) for k in range(1, side)])
-        if buffer is xs:
-            pass_on(0, xs)
-
-    def finish_gather(number, buffer):
-        for k in range(1, side):
-            from_b[number][k - 1].wait_recv()
-            got = buffer.at[core, block_of(a, turn(b, -k, side))]
+        from_dp.append([send(own, own, peer_dp(k)) for k in range(1, n_dp)])
+
+    def pass_on(number, buffer):
+        for k in range(1, n_dp):
+            from_dp[number][k - 1].wait_recv()
+            got = buffer.at[core, turn(dp, -k, n_dp)]
             from_core[number].append(send(got, got, sibling))
-        for k in range(1, side):
-            for m in range(1, side):
-                from_ab[number][(k - 1) * (side - 1) + m - 1].wait_recv()
-                got = buffer.at[core, block_of(turn(a, -k, side), turn(b, -m, side))]
-                from_core[number].append(send(got, got, sibling))
 
     def whole(buffer, part):
         return buffer[part].reshape(n_dp * rows, half)
@@ -146,12 +114,11 @@
         stores.append(pltpu.make_async_copy(source, target, store_sem.at[len(stores)]))
         stores[-1].start()
 
-    finish_gather(0, xs)
+    pass_on(0, xs)
     for copy in from_core[0]:
         copy.wait_recv()
     loads[0].wait()
     gate[...] = dot(wg[:, :half], whole(xs, 0), 1, 1) + dot(wg[:, half:], whole(xs, 1), 1, 1)
-    pass_on(1, ds)
     loads[1].wait()
     up[...] = dot(wu[:, :half], whole(xs, 0), 1, 1) + dot(wu[:, half:], whole(xs, 1), 1, 1)
     hid = gate.shape[0]
@@ -213,34 +180,15 @@
             if acc[q].shape[2] > wide:
                 sb[q][block, :, wide:] = acc[q][block, :, wide:].astype(BF16)
 
-        copies = []
-        for k in range(1, side):
-            for m in range(side):
-                source = sb[q].at[block_of(turn(a, k, side), m)]
-                copies.append(send(source, ra[q].at[k - 1, m], peer_a(k)))
-        return copies
-
-    def first_done(q, copies):
-        for copy in copies:
-            copy.wait_recv()
-        following = []
-        for m in range(1, side + 1):
-            goal = turn(b, m, side)
-            total = acc[q][block_of(a, goal)]
-            for k in range(1, side):
-                total = total + ra[q][k - 1, goal].astype(F32)
-            if m < side:
-                sc[q][m - 1] = total.astype(BF16)
-                following.append(send(sc[q].at[m - 1], rb[q].at[m - 1], peer_b(m)))
-            else:
-                acc[q][block_of(a, b)] = total
-        return following
+        return [
+            send(sb[q].at[turn(dp, k, n_dp)], rb[q].at[k - 1], peer_dp(k)) for k in range(1, n_dp)
+        ]
 
     def second_done(q, copies):
         for copy in copies:
             copy.wait_recv()
-        total = acc[q][block_of(a, b)]
-        for k in range(1, side):
+        total = acc[q][dp]
+        for k in range(1, n_dp):
             total = total + rb[q][k - 1].astype(F32)
         high, wide = zb[q].shape[1:]
         for part in range(n_z):
@@ -262,7 +210,13 @@
         ag[q][core, z] = total.astype(BF16)
         own = ag[q].at[core, z]
         following = [send(own, own, peer_z(k)) for k in range(1, n_z)]
-        return following, [send(own, own, sibling)]
+        shared = [send(own, own, sibling)]
+        if q > 0:
+            for k in range(1, n_z):
+                other = turn(z, k, n_z) * CORES + 1 - core
+                shared.append(send(own, own, (dp, other)))
+            shared += following
+        return following, shared
 
     def fourth_done(q, copies, shared):
         for k in range(1, n_z):
@@ -272,7 +226,7 @@
 
     loads[2].wait()
     pair0 = other_half(0)
-    finish_gather(1, ds)
+    pass_on(1, ds)
     own_half(0)
     step0 = pair_done(0, pair0)
     for copy in from_core[1]:
@@ -305,27 +259,22 @@
         acc[1][:, :, wide + 128 :] = jnp.zeros((n_dp, rows, extra), F32)
 
     pair1 = other_half(1)
-    step0 = first_done(0, step0)
     own_half(1)
     step1 = pair_done(1, pair1)
     pair2 = other_half(2)
     step0 = second_done(0, step0)
     own_half(2)
     step2 = pair_done(2, pair2)
-    step1 = first_done(1, step1)
+    step1 = second_done(1, step1)
     keep(xs, xs_out)
     keep(ds, ds_out)
     for source, target in zip(turned, (hw_out, dg_out, du_out)):
         keep(source, target)
     step0, shared0 = third_done(0, step0)
-    step2 = first_done(2, step2)
-    step1 = second_done(1, step1)
     step2 = second_done(2, step2)
+    unused, shared1 = third_done(1, step1)
     fourth_done(0, step0, shared0)
-    step1, shared1 = third_done(1, step1)
-    step2, shared2 = third_done(2, step2)
-    fourth_done(1, step1, shared1)
-    fourth_done(2, step2, shared2)
+    unused, shared2 = third_done(2, step2)
 
     for q, (target, shared) in enumerate(
         ((mixed_out, shared0), (dtok_out, shared1), (dtok_out, shared2))
@@ -356,24 +305,29 @@
 
 def finish(
     tile, route, mixed, d_tokens, xs, ds, hw, dg, du, route_out, mixed_out, dtok_out, gg, gu, gd,
-    x_in, d_in, hw_in, dg_in, du_in, stage, load_sem, store_sem,
+    x_in, d_in, hw_in, dg_in, du_in, m_in, t_in, stage, load_sem, store_sem,
 ):
     def copy(source, target, sem):
         made = pltpu.make_async_copy(source, target, sem)
         made.start()
         return made
 
-    moves = ((hw, hw_in), (ds, d_in), (dg, dg_in), (xs, x_in), (du, du_in))
+    moves = (
+        (hw, hw_in), (ds, d_in), (mixed, m_in), (d_tokens, t_in), (dg, dg_in), (xs, x_in), (du, du_in)
+    )
     loads = [copy(source, target, load_sem.at[k]) for k, (source, target) in enumerate(moves)]
-    stores = [copy(mixed, mixed_out, store_sem.at[0]), copy(d_tokens, dtok_out, store_sem.at[1])]
+    stores = []
     route_out[...] = jnp.transpose(route[...])[: route_out.shape[0]]
     half = xs.shape[3]
     total_rows = hw.shape[1]
     for number, (left, buffer, target, ready) in enumerate(
-        ((hw_in, d_in, gd, 2), (dg_in, x_in, gg, 2), (du_in, x_in, gu, 1))
+        ((hw_in, d_in, gd, 2), (dg_in, x_in, gg, 4), (du_in, x_in, gu, 1))
     ):
         for _ in range(ready):
             loads.pop(0).wait()
+        if number == 1:
+            stores.append(copy(m_in, mixed_out, store_sem.at[0]))
+            stores.append(copy(t_in, dtok_out, store_sem.at[1]))
         for part in range(CORES):
 
             @pl.loop(0, half // tile)
@@ -398,7 +352,6 @@
 def body(tokens, d_mixed, route_ids, route_weight, gate_weight, up_weight, down_weight):
     n_dp = lax.axis_size("dp")
     n_z = lax.axis_size("expert") // CORES
-    side = math.isqrt(n_dp)
     rows, width = tokens.shape
     choices = route_ids.shape[1]
     hid = gate_weight.shape[1]
@@ -428,15 +381,13 @@
     scratch += each(lambda w: vmem(n_dp, rows, w), plain_widths) * 2
     scratch += each(lambda w: vmem(n_dp, rows, w, dtype=F32))
     scratch += each(lambda w: vmem(n_dp, rows, w))
-    scratch += each(lambda w: vmem(side - 1, side, rows, w))
-    scratch += each(lambda w: vmem(side - 1, rows, w))
-    scratch += each(lambda w: vmem(side - 1, rows, w))
+    scratch += each(lambda w: vmem(n_dp - 1, rows, w))
     scratch += each(lambda w: vmem(n_z, high, w // col_parts))
     scratch += each(lambda w: vmem(n_z, high, w // col_parts, dtype=F32))
     scratch += each(lambda w: vmem(n_z - 1, high, w // col_parts))
     scratch += each(lambda w: vmem(CORES, n_z, high, w // col_parts))
-    gather = 2 * (2 * (side - 1) + (side - 1) ** 2 + n_dp - 1)
-    reduce = len(chunks) * (1 + (side - 1) * side + side - 1 + 2 * (n_z - 1) + n_z)
+    gather = 4 * (n_dp - 1)
+    reduce = len(chunks) * (n_dp + 3 * n_z - 2)
     copies = gather + reduce
     scratch += [pltpu.SemaphoreType.DMA((copies,))] * 2
     scratch += [pltpu.SemaphoreType.DMA((3,)), pltpu.SemaphoreType.DMA((5,))]
@@ -446,7 +397,7 @@
     flat = jax.ShapeDtypeStruct((rows, width), BF16)
     gathered = jax.ShapeDtypeStruct((CORES, n_dp, rows, half), BF16)
     left = jax.ShapeDtypeStruct((hid, total_rows), BF16)
-    shape = (n_dp, side, n_z, rows, half, row_parts, tile, chunks)
+    shape = (n_dp, n_z, rows, half, row_parts, tile, chunks)
     results = pl.pallas_call(
         functools.partial(kernel, shape),
         out_shape=(flat, jax.ShapeDtypeStruct((rows, 128), F32), flat)
@@ -473,7 +424,8 @@
         out_specs=(in_vmem,) + (anywhere,) * 5,
         scratch_shapes=[vmem(CORES, n_dp, rows, half)] * 2
         + [vmem(hid, total_rows)] * 3
-        + [vmem(3, hid, width), pltpu.SemaphoreType.DMA((5,)), pltpu.SemaphoreType.DMA((8,))],
+        + [vmem(rows, width)] * 2
+        + [vmem(3, hid, width), pltpu.SemaphoreType.DMA((7,)), pltpu.SemaphoreType.DMA((8,))],
         compiler_params=pltpu.CompilerParams(vmem_limit_bytes=60 * 1024 * 1024),
         cost_estimate=pl.CostEstimate(
             flops=6 * total_rows * hid * width,

time: 71.7 us -> 60.2 us (0.84)
  Pallas kernels: 70.9 us -> 59.4 us
    pallas_call x1, Pallas kernels: 18.5 us -> 8.13 us  [body(): pl.pallas_call(functools.partial(finish, 2 * tile), out_shape=(jax.ShapeD...]
    pallas_call x1, Pallas kernels: 52.4 us -> 51.2 us  [body(): pl.pallas_call(functools.partial(kernel, shape), out_shape=(flat, jax.Sha...]
where the time goes in v4:
time: 60.2 us; the launch traced here: 60 us
  Pallas kernels  59.4 us (99%)
  between operations  0.64 us (1%)
    pallas_call x1, Pallas kernels, body(): pl.pallas_call(functools.partial(kernel, shape), out_shape=(flat, jax.Sha...  51.2 us
    pallas_call x1, Pallas kernels, body(): pl.pallas_call(functools.partial(finish, 2 * tile), out_shape=(jax.ShapeD...  8.13 us

profile of v4, /device:TPU:0, one launch (start us, length us, event | category | flops | bytes accessed | tf_op | source)
XLA Modules:
  0.0 60.0 jit_solution(16014096723908369540)
XLA Ops:
  0.6 51.2 %shard_map.118 = (bf16[64,2048]{1,0:T(8,128)(2,1)}, f32[64,128]{1,0:T(8,128)}, bf16[64,2048]{1,0:T(8,128)(2,1)}, bf16[2,4,64,1024]{3,2,1,0:T(8,128)(2,1)}, bf16[...) custom-call(bf16[64,2048]{1,0:T(8,128)(2,1)} %tok.1, ...), custom_call_target="tpu_custom_call" | custom-call | flops 4429185024 | bytes 8650752 | tf_op jit(solution)/shard_map/pallas_call | solution.py:401
  51.9 8.1 %shard_map.119 = (f32[6,64]{1,0:T(8,128)}, bf16[64,2048]{1,0:T(8,128)(2,1)}, bf16[64,2048]{1,0:T(8,128)(2,1)}, bf16[1,704,2048]{2,1,0:T(8,128)(2,1)}, bf16[1,704...) custom-call(f32[64,128]{1,0:T(8,128)} %get-tuple-element.20.route, bf16[64,2048]{1,0:T(8,128)(2,1)} %get-tuple-element.21.mixed, ...), custom_call_target="tpu_custom_call" | custom-call | flops 2214592512 | bytes 8650752 | tf_op jit(solution)/shard_map/pallas_call | solution.py:420

commit v5 on v4

--- a/solution.py
+++ b/solution.py
@@ -211,11 +211,6 @@
         own = ag[q].at[core, z]
         following = [send(own, own, peer_z(k)) for k in range(1, n_z)]
         shared = [send(own, own, sibling)]
-        if q > 0:
-            for k in range(1, n_z):
-                other = turn(z, k, n_z) * CORES + 1 - core
-                shared.append(send(own, own, (dp, other)))
-            shared += following
         return following, shared
 
     def fourth_done(q, copies, shared):
@@ -272,9 +267,11 @@
         keep(source, target)
     step0, shared0 = third_done(0, step0)
     step2 = second_done(2, step2)
-    unused, shared1 = third_done(1, step1)
+    step1, shared1 = third_done(1, step1)
     fourth_done(0, step0, shared0)
-    unused, shared2 = third_done(2, step2)
+    step2, shared2 = third_done(2, step2)
+    fourth_done(1, step1, shared1)
+    fourth_done(2, step2, shared2)
 
     for q, (target, shared) in enumerate(
         ((mixed_out, shared0), (dtok_out, shared1), (dtok_out, shared2))

time: 60.2 us -> 59.6 us (0.990)
  Pallas kernels: 59.4 us -> 58.7 us
    pallas_call x1, Pallas kernels: 51.2 us -> 50.6 us  [body(): pl.pallas_call(functools.partial(kernel, shape), out_shape=(flat, jax.Sha...]
where the time goes in v5:
time: 59.6 us; the launch traced here: 59.4 us
  Pallas kernels  58.7 us (98%)
  between operations  0.64 us (1%)
    pallas_call x1, Pallas kernels, body(): pl.pallas_call(functools.partial(kernel, shape), out_shape=(flat, jax.Sha...  50.6 us
    pallas_call x1, Pallas kernels, body(): pl.pallas_call(functools.partial(finish, 2 * tile), out_shape=(jax.ShapeD...  8.15 us

profile of v5, /device:TPU:0, one launch (start us, length us, event | category | flops | bytes accessed | tf_op | source)
XLA Modules:
  0.0 59.4 jit_solution(11260666654620181992)
XLA Ops:
  0.6 50.6 %shard_map.118 = (bf16[64,2048]{1,0:T(8,128)(2,1)}, f32[64,128]{1,0:T(8,128)}, bf16[64,2048]{1,0:T(8,128)(2,1)}, bf16[2,4,64,1024]{3,2,1,0:T(8,128)(2,1)}, bf16[...) custom-call(bf16[64,2048]{1,0:T(8,128)(2,1)} %tok.1, ...), custom_call_target="tpu_custom_call" | custom-call | flops 4429185024 | bytes 8650752 | tf_op jit(solution)/shard_map/pallas_call | solution.py:398
  51.2 8.1 %shard_map.119 = (f32[6,64]{1,0:T(8,128)}, bf16[64,2048]{1,0:T(8,128)(2,1)}, bf16[64,2048]{1,0:T(8,128)(2,1)}, bf16[1,704,2048]{2,1,0:T(8,128)(2,1)}, bf16[1,704...) custom-call(f32[64,128]{1,0:T(8,128)} %get-tuple-element.20.route, bf16[64,2048]{1,0:T(8,128)(2,1)} %get-tuple-element.21.mixed, ...), custom_call_target="tpu_custom_call" | custom-call | flops 2214592512 | bytes 8650752 | tf_op jit(solution)/shard_map/pallas_call | solution.py:417

commit v6 on v5

--- a/solution.py
+++ b/solution.py
@@ -353,7 +353,7 @@
     choices = route_ids.shape[1]
     hid = gate_weight.shape[1]
     half = width // CORES
-    tile = 256
+    tile = 512
     row_parts = min(n_z, rows // 16)
     col_parts = n_z // row_parts
     high = rows // row_parts

time: 59.6 us -> 57.1 us (0.958)
  Pallas kernels: 58.7 us -> 56.3 us
    pallas_call x1, Pallas kernels: 8.15 us -> 6.92 us  [body(): pl.pallas_call(functools.partial(finish, 2 * tile), out_shape=(jax.ShapeD...]
    pallas_call x1, Pallas kernels: 50.6 us -> 49.4 us  [body(): pl.pallas_call(functools.partial(kernel, shape), out_shape=(flat, jax.Sha...]
where the time goes in v6:
time: 57.1 us; the launch traced here: 56.9 us
  Pallas kernels  56.3 us (99%)
  between operations  0.64 us (1%)
    pallas_call x1, Pallas kernels, body(): pl.pallas_call(functools.partial(kernel, shape), out_shape=(flat, jax.Sha...  49.4 us
    pallas_call x1, Pallas kernels, body(): pl.pallas_call(functools.partial(finish, 2 * tile), out_shape=(jax.ShapeD...  6.92 us

profile of v6, /device:TPU:0, one launch (start us, length us, event | category | flops | bytes accessed | tf_op | source)
XLA Modules:
  0.0 56.9 jit_solution(7309566823422857178)
XLA Ops:
  0.6 49.4 %shard_map.118 = (bf16[64,2048]{1,0:T(8,128)(2,1)}, f32[64,128]{1,0:T(8,128)}, bf16[64,2048]{1,0:T(8,128)(2,1)}, bf16[2,4,64,1024]{3,2,1,0:T(8,128)(2,1)}, bf16[...) custom-call(bf16[64,2048]{1,0:T(8,128)(2,1)} %tok.1, ...), custom_call_target="tpu_custom_call" | custom-call | flops 4429185024 | bytes 8650752 | tf_op jit(solution)/shard_map/pallas_call | solution.py:398
  50.0 6.9 %shard_map.119 = (f32[6,64]{1,0:T(8,128)}, bf16[64,2048]{1,0:T(8,128)(2,1)}, bf16[64,2048]{1,0:T(8,128)(2,1)}, bf16[1,704,2048]{2,1,0:T(8,128)(2,1)}, bf16[1,704...) custom-call(f32[64,128]{1,0:T(8,128)} %get-tuple-element.20.route, bf16[64,2048]{1,0:T(8,128)(2,1)} %get-tuple-element.21.mixed, ...), custom_call_target="tpu_custom_call" | custom-call | flops 2214592512 | bytes 8650752 | tf_op jit(solution)/shard_map/pallas_call | solution.py:417
